TPU v7x, 256 devices: a whole 4x4x8 slice. The times are simulated.
256 devices in a mesh: ctx: 32 (over x, z), head: 8 (over y, core).
Axes of the slice: x: 4, y: 4, z: 8, core: 2. Of those that a mesh axis runs over, the one named last changes fastest.
Arguments:
- tokens: bfloat16 [256, 4096], P(None, 'ctx'), may hold values from -400 to 400
- input_norm_gain: bfloat16 [4096], P('ctx'), may hold values from 0.099609375 to 1.8984375
- query_matrix: bfloat16 [4096, 4096], P('ctx', 'head'), may hold values from -0.09375 to 0.09375
- key_matrix: bfloat16 [4096, 1024], P('ctx', 'head'), may hold values from -0.09375 to 0.09375
- value_matrix: bfloat16 [4096, 1024], P('ctx', 'head'), may hold values from -0.09375 to 0.09375
- output_matrix: bfloat16 [4096, 4096], P('head', 'ctx'), may hold values from -0.09375 to 0.09375
- cached_key_rows: bfloat16 [262144, 1024], P('ctx', 'head'), may hold values from -64 to 64
- cached_value_rows: bfloat16 [262144, 1024], P('ctx', 'head'), may hold values from -6 to 6
- cache_block_recording: int32 [2048], P('ctx'), may hold values from 0 to 63, never falling along the last dimension, each value on 1 to 128 neighbouring positions
- stretch_token_recording: int32 [256], replicated, may hold values from 0 to 63, never falling along the last dimension, each value on 1 to 16 neighbouring positions
- adapter_down_store: bfloat16 [64, 64, 4096], P('ctx'), may hold values from -0.09375 to 0.09375
- adapter_up_store: bfloat16 [64, 64, 4096], P('ctx', None, 'head'), may hold values from -0.75 to 0.75
- adapter_store_slot: int32 [64], replicated, may hold values from 0 to 63, each once
- adapter_wanted_list: int32 [4], replicated, may hold values from 0 to 63, as said below
- token_adapter_place: int32 [256], replicated, may hold values from 0 to 3
Outputs:
- mixed_out: bfloat16 [256, 4096], P('head', 'ctx')
Inputs may be any that keep to these rules, and one draw needn't show every extreme that they name: `cache_block_recording`: the recording of each block of 128 cache tokens; it never falls along the cache and every recording has at least one block. `stretch_token_recording`: never falls along the stretch and every recording has at least one stretch token. `adapter_store_slot`: store slot s lies at ctx index s // 2, place s % 2 of that index's store; every slot once. `adapter_wanted_list`: distinct adapter ids.
All inputs are finite; a program needn't handle non-finite values.
Results may differ from a plain program's by a relative error of at most 0.011.
The roundings to bfloat16 on the way count: a program that leaves them out, or rounds other values in their place, can miss the bound.
Values may be sent and summed in bfloat16 or wider, within the bound.
No kernel may reach another device: no remote copies, remote signals or barrier semaphores. Data moves between devices by JAX's collectives and lax.ppermute only.
A program may use at most 64 MiB of HBM per device.

v0:
```python
import math

import jax
import jax.numpy as jnp
from jax import lax
from jax.sharding import PartitionSpec as P

MODEL_WIDTH = 4096
HEAD_WIDTH = 128
SPAN = 128
NEED = 4
GROUP = 4


NEGATIVE = -1e30
EPSILON = 1e-05
ADAPTER_SCALE = 0.5


def spread(block, axis, owner):
    block = jnp.where(lax.axis_index(axis) == owner, block, jnp.zeros_like(block))
    return lax.psum(block, axis)


def joined(part, axis, combine):
    gathered = jax.tree.map(lambda a: lax.all_gather(a, axis), part)

    def take(source):
        return jax.tree.map(lambda a: lax.dynamic_index_in_dim(a, source, 0, False), gathered)

    return lax.fori_loop(
        1, lax.axis_size(axis), lambda source, state: combine(state, take(source)), take(0)
    )


def attend(carried, query_tile, key_block, value_block, allowed):
    highest, mass_sum, numerator = carried
    scores = jnp.einsum(
        "qhgd,khd->hgqk", query_tile, key_block, preferred_element_type=jnp.float32
    ) * (1.0 / math.sqrt(HEAD_WIDTH))
    scores = jnp.where(allowed[None, None], scores, NEGATIVE)
    peak_new = jnp.maximum(highest, jnp.max(scores, axis=-1))
    factor = jnp.exp(highest - peak_new)
    weights = jnp.where(allowed[None, None], jnp.exp(scores - peak_new[..., None]), 0.0)
    mass_sum = mass_sum * factor + jnp.sum(weights, axis=-1)
    numerator = numerator * jnp.transpose(factor, (2, 0, 1))[..., None] + jnp.einsum(
        "hgqk,khd->qhgd",
        weights.astype(jnp.bfloat16),
        value_block,
        preferred_element_type=jnp.float32,
    )
    return (peak_new, mass_sum, numerator)


def update_rows(carried, first_row, length, query_heads, key_block, value_block, allowed, active):
    last_row = first_row + length
    tile_state = (
        carried[0][:, :, first_row:last_row],
        carried[1][:, :, first_row:last_row],
        carried[2][first_row:last_row],
    )
    tile_queries = query_heads[first_row:last_row]

    def attend_tile(inner_state):
        return attend(inner_state, tile_queries, key_block, value_block, allowed)

    def keep_state(inner_state):
        return inner_state

    if active is None:
        tile_state = attend_tile(tile_state)
    else:
        tile_state = lax.cond(active, attend_tile, keep_state, tile_state)
    return (
        carried[0].at[:, :, first_row:last_row].set(tile_state[0]),
        carried[1].at[:, :, first_row:last_row].set(tile_state[1]),
        carried[2].at[first_row:last_row].set(tile_state[2]),
    )


def finish_queries(query_total, middle_sum, inverse_root_square, slots, up_map_list):
    middle = (middle_sum * inverse_root_square[:, None]).astype(jnp.bfloat16)
    query_change = jnp.zeros(query_total.shape, jnp.float32)
    for wanted_index, up_table in enumerate(up_map_list):
        product = jnp.dot(middle, up_table, preferred_element_type=jnp.float32)
        query_change = query_change + jnp.where((slots == wanted_index)[:, None], product, 0.0)
    return (query_total * inverse_root_square[:, None] + ADAPTER_SCALE * query_change).astype(
        jnp.bfloat16
    )


def join_states(first_state, second_state):
    total_rows, head_count = first_state[0].shape
    highest = jnp.maximum(first_state[0], second_state[0])
    first_weight = jnp.exp(first_state[0] - highest)
    second_weight = jnp.exp(second_state[0] - highest)
    mass_sum = first_state[1] * first_weight + second_state[1] * second_weight
    numerator = (
        first_state[2].reshape(total_rows, head_count, HEAD_WIDTH) * first_weight[..., None]
        + second_state[2].reshape(total_rows, head_count, HEAD_WIDTH) * second_weight[..., None]
    )
    return (highest, mass_sum, numerator.reshape(total_rows, head_count * HEAD_WIDTH))


def normalize(mass_sum, numerator):
    total_rows, head_count = mass_sum.shape
    return (
        (numerator.reshape(total_rows, head_count, HEAD_WIDTH) / mass_sum[..., None])
        .reshape(total_rows, head_count * HEAD_WIDTH)
        .astype(jnp.bfloat16)
    )


def shards(
    tokens,
    input_norm_gain,
    query_matrix,
    key_matrix,
    value_matrix,
    output_matrix,
    cached_key_rows,
    cached_value_rows,
    cache_block_recording,
    stretch_token_recording,
    adapter_down_store,
    adapter_up_store,
    adapter_store_slot,
    adapter_wanted_list,
    token_adapter_place,
):
    total_rows = tokens.shape[0]
    columns = tokens.shape[1]
    ctx_count = lax.axis_size("ctx")
    ctx_index = lax.axis_index("ctx")
    own_count = total_rows // ctx_count
    own_start = ctx_index * own_count
    float_tokens = tokens.astype(jnp.float32)
    squares = jnp.sum(float_tokens * float_tokens, axis=1)
    scaled_change = (float_tokens * input_norm_gain.astype(jnp.float32)).astype(jnp.bfloat16)
    query_part = jnp.dot(scaled_change, query_matrix, preferred_element_type=jnp.float32)
    key_part = jnp.dot(scaled_change, key_matrix, preferred_element_type=jnp.float32)
    value_part = jnp.dot(scaled_change, value_matrix, preferred_element_type=jnp.float32)
    device_portion = adapter_down_store.shape[0]
    home_slot = adapter_store_slot[adapter_wanted_list]
    home_device = home_slot // device_portion
    device_local_index = home_slot % device_portion
    middle_product = jnp.zeros((total_rows, adapter_down_store.shape[1]), jnp.float32)
    up_map_list = []
    for wanted_index in range(NEED):
        down_map_part = lax.dynamic_index_in_dim(
            adapter_down_store, device_local_index[wanted_index], 0, keepdims=False
        )
        up_map_part = lax.dynamic_index_in_dim(
            adapter_up_store, device_local_index[wanted_index], 0, keepdims=False
        )
        fetched = (
            spread(down_map_part, "ctx", home_device[wanted_index]),
            spread(up_map_part, "ctx", home_device[wanted_index]),
        )
        down_rows = lax.dynamic_slice_in_dim(fetched[0], ctx_index * columns, columns, 1)
        product = lax.dot_general(
            scaled_change, down_rows, (((1,), (1,)), ((), ())), preferred_element_type=jnp.float32
        )
        middle_product = middle_product + jnp.where(
            (token_adapter_place == wanted_index)[:, None], product, 0.0
        )
        up_map_list.append(fetched[1])
    query_total, middle_sum, square_sum = lax.psum((query_part, middle_product, squares), "ctx")
    key_sum, value_sum = (
        lax.psum_scatter(key_part, "ctx", scatter_dimension=0, tiled=True),
        lax.psum_scatter(value_part, "ctx", scatter_dimension=0, tiled=True),
    )
    inverse_all = lax.rsqrt(square_sum / MODEL_WIDTH + EPSILON)
    query_vectors = finish_queries(
        query_total, middle_sum, inverse_all, token_adapter_place, up_map_list
    )
    inverse_own = lax.dynamic_slice_in_dim(inverse_all, own_start, own_count, 0)
    new_keys = (key_sum * inverse_own[:, None]).astype(jnp.bfloat16)
    new_values = (value_sum * inverse_own[:, None]).astype(jnp.bfloat16)
    heads_kv = cached_key_rows.shape[1] // HEAD_WIDTH
    tile_len = min(128, total_rows)
    tile_count = total_rows // tile_len
    block_len = min(512, cached_key_rows.shape[0])
    block_count = cached_key_rows.shape[0] // block_len
    query_heads = query_vectors.reshape(total_rows, heads_kv, GROUP, HEAD_WIDTH)
    key_blocks = cached_key_rows.reshape(block_count, block_len, heads_kv, HEAD_WIDTH)
    value_blocks = cached_value_rows.reshape(block_count, block_len, heads_kv, HEAD_WIDTH)
    record_blocks = jnp.repeat(cache_block_recording, SPAN).reshape(block_count, block_len)
    carried = (
        jnp.full((heads_kv, GROUP, total_rows), NEGATIVE, jnp.float32),
        jnp.zeros((heads_kv, GROUP, total_rows), jnp.float32),
        jnp.zeros((total_rows, heads_kv, GROUP, HEAD_WIDTH), jnp.float32),
    )

    def cache_step(carry_in, blocks):
        key_block, value_block, record_block = blocks
        for tile_index in range(tile_count):
            first_row = tile_index * tile_len
            query_records = stretch_token_recording[first_row : first_row + tile_len]
            active = (query_records[0] <= record_block[-1]) & (record_block[0] <= query_records[-1])
            allowed = query_records[:, None] == record_block[None, :]
            carry_in = update_rows(
                carry_in, first_row, tile_len, query_heads, key_block, value_block, allowed, active
            )
        return (carry_in, None)

    carried, unused = lax.scan(cache_step, carried, (key_blocks, value_blocks, record_blocks))
    key_positions = own_start + jnp.arange(own_count, dtype=jnp.int32)
    key_records = lax.dynamic_slice_in_dim(stretch_token_recording, own_start, own_count, 0)
    stretch_keys = new_keys.reshape(own_count, heads_kv, HEAD_WIDTH)
    stretch_values = new_values.reshape(own_count, heads_kv, HEAD_WIDTH)
    for tile_index in range(tile_count):
        first_row = tile_index * tile_len
        query_positions = first_row + jnp.arange(tile_len, dtype=jnp.int32)
        query_records = stretch_token_recording[first_row : first_row + tile_len]
        allowed = (query_records[:, None] == key_records[None, :]) & (
            key_positions[None, :] <= query_positions[:, None]
        )
        carried = update_rows(
            carried, first_row, tile_len, query_heads, stretch_keys, stretch_values, allowed, None
        )
    highest, mass_sum, numerator = carried
    flat_peak = jnp.transpose(highest, (2, 0, 1)).reshape(total_rows, heads_kv * GROUP)
    flat_mass = jnp.transpose(mass_sum, (2, 0, 1)).reshape(total_rows, heads_kv * GROUP)
    flat_numerator = numerator.reshape(total_rows, heads_kv * GROUP * HEAD_WIDTH)
    merged = joined((flat_peak, flat_mass, flat_numerator), "ctx", join_states)
    attention = normalize(merged[1], merged[2])
    mixed_out = lax.psum_scatter(
        jnp.dot(attention, output_matrix, preferred_element_type=jnp.float32),
        "head",
        scatter_dimension=0,
        tiled=True,
    )
    return mixed_out.astype(jnp.bfloat16)


def solution(mesh):
    in_specs = (
        P(None, "ctx"),
        P("ctx"),
        P("ctx", "head"),
        P("ctx", "head"),
        P("ctx", "head"),
        P("head", "ctx"),
        P("ctx", "head"),
        P("ctx", "head"),
        P("ctx"),
        P(),
        P("ctx", None, None),
        P("ctx", None, "head"),
        P(),
        P(),
        P(),
    )
    out_specs = P("head", "ctx")
    return jax.shard_map(shards, mesh=mesh, in_specs=in_specs, out_specs=out_specs, check_vma=False)
```

profile of v0, /device:TPU:1, one launch (start us, length us, event | category | flops | bytes accessed | tf_op | source)
XLA Modules:
  0.0 737.6 jit_solution(326464489429285962)
XLA Ops:
  19.7 1.7 select_bitcast_fusion.7
  21.4 1.4 select_bitcast_fusion
  26.3 152.7 %all-reduce.9.cloned.1.call-done = (bf16[64,4096]{1,0:T(8,128)(2,1)}, bf16[64,4096]{1,0:T(8,128)(2,1)}, bf16[64,4096]{1,0:T(8,128)(2,1)}, bf16[64,4096]{1,0:T(8,...) async-done(((bf16[64,4096]{1,0:T(8,128)(2,1)}, bf16[64,4096]{1,0:T(8,128)(2,1)}, ...) | async-done | bytes 2359312 | tf_op jit(solution)/shard_map/psum | solution.py:22
  181.7 1.5 fusion.45
  183.4 58.2 %psum.78 = f32[256]{0:T(256)S(1)} all-reduce(f32[256]{0:T(256)S(1)} %fusion.56), channel_id=1, replica_groups=mesh['ctx'=32,'head'=8] {'ctx'}, use_global_device_ids=true, to_apply=%region_2.3 | all-reduce | flops 256 | bytes 2048 | tf_op jit(solution)/shard_map/psum | solution.py:168
  243.1 85.8 %all-reduce.7.cloned.1.call-done = (f32[256,64]{0,1:T(8,128)}, f32[256,512]{1,0:T(8,128)}, f32[256,128]{1,0:T(8,128)}, f32[256,128]{1,0:T(8,128)}) async-done(((f32[256,64]{0,1:T(8,128)}, f32[256,512]{1,0:T(8,128)}, f32[256,128]{1,0:T(8,128)}, f32[256,128]{1,0:T(8,128)}), (f32[256,64]{0,1:T(8,128)}, f32[256,512]{1,0:T(8,128)}, f32[256,128]{1,0:T(8,128)}, f32[256,128]{1,0:T(8,128)})) %all-reduce.7.cloned.1.call-update) | async-done | bytes 851984 | tf_op jit(solution)/shard_map/psum | solution.py:168
  332.0 141.1 %while.48 = (s32[]{:T(128)}, f32[1,4,256]{2,1,0:T(4,128)S(1)}, f32[1,4,256]{2,1,0:T(4,128)S(1)}, f32[256,1,4,128]{3,0,2,1:T(8,128)S(1)}, s32[256]{0:T(256)S(1)},...) while((s32[]{:T(128)}, f32[1,4,256]{2,1,0:T(4,128)S(1)}, ...), condition=%wide.region_21.22_spmd, body=%wide.region_12.21_spmd.sunk | while | flops 273550336 | bytes 12166637 | solution.py:207
  478.3 38.3 %all-gather = f32[8192,1,4]{0,2,1:T(4,128)S(1)} all-gather(f32[256,1,4]{0,2,1:T(4,128)S(1)} %bitcast.296), channel_id=2, replica_groups=mesh['ctx'=32,'head'=8] {'ctx'}, dimensions={0}, use_global_device_ids=true | all-gather | bytes 135168 | tf_op jit(solution)/shard_map/all_gather | solution.py:26
  516.6 32.5 %all-gather.1 = f32[8192,1,4]{0,2,1:T(4,128)S(1)} all-gather(f32[256,1,4]{0,2,1:T(4,128)S(1)} %bitcast.297), channel_id=3, replica_groups=mesh['ctx'=32,'head'=8] {'ctx'}, dimensions={0}, use_global_device_ids=true | all-gather | bytes 135168 | tf_op jit(solution)/shard_map/all_gather | solution.py:26
  549.1 76.1 %all-gather.4.cloned.1.call-done = f32[32,256,512]{2,1,0:T(8,128)} async-done(((f32[1,256,512]{2,1,0:T(8,128)}), f32[32,256,512]{2,1,0:T(8,128)}) %all-gather.4.cloned.1.call-update) | async-done | bytes 16777232 | tf_op jit(solution)/shard_map/all_gather | solution.py:26
  626.3 74.1 %while.49 = (s32[]{:T(128)}, f32[256,4]{0,1:T(4,128)S(1)}, f32[256,4]{0,1:T(4,128)S(1)}, f32[256,512]{1,0:T(8,128)S(1)}, f32[32,256,4]{1,2,0:T(4,128)S(1)}, /*in...) while((s32[]{:T(128)}, f32[256,4]{0,1:T(4,128)S(1)}, ...), condition=%wide.region_29.30_spmd, body=%wide.region_28.29_spmd.sunk | while | flops 399365 | bytes 3727503 | solution.py:31
  627.3 1.4 fusion.133
  629.7 1.4 fusion.133
  632.1 1.4 fusion.133
  634.5 1.4 fusion.133
  646.4 1.4 fusion.133
  653.6 1.4 fusion.133
  660.8 1.4 fusion.133
  665.5 1.4 fusion.133
  672.7 1.4 fusion.133
  679.9 1.4 fusion.133
  691.8 1.4 fusion.133
  699.0 1.4 fusion.133
  701.8 27.9 %reduce-scatter.2.cloned.1.call-done = f32[32,128]{1,0:T(8,128)} async-done(((f32[256,128]{1,0:T(8,128)}), f32[32,128]{1,0:T(8,128)}) %reduce-scatter.2.cloned.1.call-update) | async-done | bytes 16400 | tf_op jit(solution)/shard_map/reduce_scatter | solution.py:228
  (698 shorter events, 153.2 us)
Async XLA Ops:
  6.5 18.7 %copy-start = (bf16[128,512]{1,0:T(8,128)(2,1)S(1)}, bf16[128,512]{1,0:T(8,128)(2,1)}, u32[]{:S(2)}) copy-start(bf16[128,512]{1,0:T(8,128)(2,1)} %param.49) | copy-start | bytes 393220
  6.5 14.8 %copy-start.1 = (bf16[2,64,4096]{2,1,0:T(8,128)(2,1)S(1)}, bf16[2,64,4096]{2,1,0:T(8,128)(2,1)}, u32[]{:S(2)}) copy-start(bf16[2,64,4096]{2,1,0:T(8,128)(2,1)} %param.57) | copy-start | bytes 3145732
  6.5 172.5 %all-reduce.9.cloned.1.call-start = ((), (), s32[]{:S(2)}) async-start(), calls=%async_computation.4 | async-start | bytes 4718592 | tf_op jit(solution)/shard_map/psum | solution.py:22
  22.8 0.7 copy-start.13
  22.8 0.7 copy-start.4
  22.8 0.8 copy-start.10
  22.8 0.9 copy-start.2
  22.8 0.9 copy-start.8
  22.8 1.7 copy-start.9
  22.8 218.8 %copy-start.11 = (s32[64]{0:T(128)S(1)}, s32[64]{0:T(128)}, u32[]{:S(2)}) copy-start(s32[64]{0:T(128)} %param.55) | copy-start | bytes 772
  22.8 219.0 %copy-start.14 = (u32[256]{0:T(256)S(1)}, u32[256]{0:T(256)}, u32[]{:S(2)}) copy-start(u32[256]{0:T(256)} %constant.502) | copy-start | bytes 3076
  22.8 306.1 %all-reduce.7.cloned.1.call-start = ((), (), s32[]{:S(2)}) async-start(), calls=%async_computation.3 | async-start | bytes 1703936 | tf_op jit(solution)/shard_map/psum | solution.py:168
  179.0 151.9 %copy-start.7 = (bf16[64,512]{1,0:T(8,128)(2,1)S(1)}, bf16[64,512]{1,0:T(8,128)(2,1)}, u32[]{:S(2)}) copy-start(bf16[64,512]{1,0:T(8,128)(2,1)} %get-tuple-element.624) | copy-start | bytes 196612
  179.0 152.2 %copy-start.6 = (bf16[64,512]{1,0:T(8,128)(2,1)S(1)}, bf16[64,512]{1,0:T(8,128)(2,1)}, u32[]{:S(2)}) copy-start(bf16[64,512]{1,0:T(8,128)(2,1)} %get-tuple-element.625) | copy-start | bytes 196612
  179.0 152.4 %copy-start.5 = (bf16[64,512]{1,0:T(8,128)(2,1)S(1)}, bf16[64,512]{1,0:T(8,128)(2,1)}, u32[]{:S(2)}) copy-start(bf16[64,512]{1,0:T(8,128)(2,1)} %get-tuple-element.626) | copy-start | bytes 196612
  183.2 442.0 %all-gather.4.cloned.1.call-start = ((), (), s32[]{:S(2)}) async-start(), calls=%async_computation.1 | async-start | bytes 17301504 | tf_op jit(solution)/shard_map/all_gather | solution.py:26
  328.9 2.5 copy-start.3
  478.2 251.5 %reduce-scatter.2.cloned.1.call-start = ((), (), s32[]{:S(2)}) async-start(), calls=%async_computation.2 | async-start | bytes 147456 | tf_op jit(solution)/shard_map/reduce_scatter | solution.py:228
  626.3 74.6 %copy-start.12 = (bf16[512,128]{1,0:T(8,128)(2,1)S(1)}, bf16[512,128]{1,0:T(8,128)(2,1)}, u32[]{:S(2)}) copy-start(bf16[512,128]{1,0:T(8,128)(2,1)} %param.52) | copy-start | bytes 393220
Sparse Core Ops, SparseCore 0:
  23.0 156.0 all-reduce.8
  183.3 145.5 all-reduce.6
  478.3 146.8 all-gather.3
  701.9 27.7 reduce-scatter.1
where the time goes:
time: 743 us; the launch traced here: 738 us
  waiting for transfers between devices  343 us (46%)
  blocking collectives  129 us (17%)
  loops' own time  85 us (11%)
  local copies, waits for them, and re-layouts  76.4 us (10%)
  other arithmetic  54.3 us (7%)
  matrix products  25.7 us (3%)
  between operations  24.4 us (3%)
    psum x1, waiting for transfers between devices, spread(): return lax.psum(block, axis)  153 us
    psum x1, waiting for transfers between devices, shards(): lax.psum((query_part, middle_product, squares), 'ctx')  85.8 us
    another operation x1, loops' own time, shards(): lax.scan(cache_step, carried, (key_blocks, value_blocks, record_blocks))  82.8 us
    all_gather x1, waiting for transfers between devices, joined(): gathered = jax.tree.map(lambda a: lax.all_gather(a, axis), part)  76.1 us
    all_gather x2, blocking collectives, joined(): gathered = jax.tree.map(lambda a: lax.all_gather(a, axis), part)  70.8 us
    psum x1, blocking collectives, shards(): lax.psum((query_part, middle_product, squares), 'ctx')  58.2 us
    add x31, other arithmetic, join_states(): first_state[2].reshape(total_rows, head_count, HEAD_WIDTH)  42.8 us
    reduce_scatter x1, waiting for transfers between devices, shards(): lax.psum_scatter(jnp.dot(attention, output_matrix, preferred_element_type...  27.9 us
  transfers between devices with their start and end apart: 4, of which 4 were waited for; matrix products, arithmetic and copies ran while one was open for 1% of the time, Pallas kernels for 0%

commit v1 on v0

v1 whole, which is shorter than its diff:
```python
import math

import jax
import jax.numpy as jnp
from jax import lax
from jax.experimental import pallas as pl
from jax.experimental.pallas import tpu as pltpu
from jax.sharding import PartitionSpec as P

MODEL_WIDTH = 4096
HEAD_WIDTH = 128
LANES = 128
SPAN = 128
NEED = 4
GROUP = 4
RANK = 64
WINDOW = 24

LOWEST = -1e30
FLOOR = -1e29
EPSILON = 1e-05
ADAPTER_SCALE = 0.5
SCORE_SCALE = math.log2(math.e) / math.sqrt(HEAD_WIDTH)

F32 = jnp.float32
BF16 = jnp.bfloat16
VMEM = pl.BlockSpec(memory_space=pltpu.VMEM)
SMEM = pl.BlockSpec(memory_space=pltpu.SMEM)


def lane_iota(shape):
    return lax.broadcasted_iota(jnp.int32, shape, len(shape) - 1)


def row_iota(shape):
    return lax.broadcasted_iota(jnp.int32, shape, len(shape) - 2)


def column_of(row):
    return jnp.transpose(jnp.broadcast_to(row.astype(F32), (LANES, LANES)))


def thirds(value):
    high = value.astype(BF16).astype(F32)
    rest = value - high
    middle = rest.astype(BF16).astype(F32)
    return high, middle, rest - middle


def contract_last(a, b):
    return lax.dot_general(a, b, (((1,), (1,)), ((), ())), preferred_element_type=F32)


def call(body, out_shape, in_specs, scratch=(), limit=16, flops=0, name=None):
    many = isinstance(out_shape, (tuple, list))
    return pl.pallas_call(
        body,
        out_shape=out_shape,
        in_specs=in_specs,
        out_specs=[VMEM] * len(out_shape) if many else VMEM,
        scratch_shapes=list(scratch),
        compiler_params=pltpu.CompilerParams(vmem_limit_bytes=limit * 1024 * 1024),
        name=name,
    )


def pack_tokens(tokens, gain, out):
    rows = out.shape[1] - 8
    first = pl.multiple_of(lax.axis_index("head") * rows, rows)
    own = tokens[pl.ds(first, rows), :].astype(F32)
    gain_rows = jnp.broadcast_to(gain[...].astype(F32), (8, LANES))
    block = jnp.concatenate([own, gain_rows], axis=0).astype(BF16)
    for target in range(out.shape[0]):
        out[target] = block


def middle_kernel(
    wanted, store_slot, blocks, down, place, stretch, cache, out, table, flat, place_columns
):
    rows = flat.shape[0]
    first_home = lax.axis_index("ctx") * 2
    squares = jnp.zeros((rows, LANES), F32)
    for source in range(blocks.shape[0]):
        block = blocks[source].astype(F32)
        token_part = block[:rows]
        squares = squares + token_part * token_part
        scaled = (token_part * block[rows : rows + 1]).astype(BF16)
        flat[:, source * LANES : (source + 1) * LANES] = scaled
    mean = jnp.sum(squares, axis=1, keepdims=True) / MODEL_WIDTH
    inverse = lax.rsqrt(mean + EPSILON)
    middle = contract_last(flat[...], down[...]) * inverse
    head = lax.axis_index("head")
    for part in range(place.shape[0]):
        place_columns[part * LANES : (part + 1) * LANES, :] = column_of(place[part : part + 1, :])
    own_place = place_columns[pl.ds(pl.multiple_of(head * rows, rows), rows), :]
    use_first = jnp.zeros((rows, LANES), jnp.bool_)
    use_second = jnp.zeros((rows, LANES), jnp.bool_)
    for wanted_index in range(NEED):
        home = store_slot[wanted[wanted_index]]
        here = own_place == float(wanted_index)
        use_first = use_first | (here & (home == first_home))
        use_second = use_second | (here & (home == first_home + 1))
    picked = jnp.where(
        use_first, middle, jnp.where(use_second, pltpu.roll(middle, RANK, 1), 0.0)
    )
    lanes = lane_iota((rows, LANES))
    high, mid, low = thirds(jnp.broadcast_to(inverse, (rows, LANES)))
    tail = jnp.where(
        lanes == RANK, high, jnp.where(lanes == RANK + 1, mid, jnp.where(lanes == RANK + 2, low, 0.0))
    )
    packed = jnp.where(lanes < RANK, picked, tail).astype(BF16)
    for target in range(out.shape[0]):
        out[target] = packed
    cache_row = jnp.broadcast_to(cache[...].astype(F32), (LANES, LANES))
    counts = [jnp.zeros((1, LANES), F32) for _ in range(2 + stretch.shape[0])]
    for part in range(stretch.shape[0]):
        column = column_of(stretch[part : part + 1, :])
        counts[0] = counts[0] + jnp.sum(jnp.where(column < cache_row, 1.0, 0.0), axis=0, keepdims=True)
        counts[1] = counts[1] + jnp.sum(jnp.where(column <= cache_row, 1.0, 0.0), axis=0, keepdims=True)
        for other in range(stretch.shape[0]):
            other_row = jnp.broadcast_to(stretch[other : other + 1, :].astype(F32), (LANES, LANES))
            counts[2 + other] = counts[2 + other] + jnp.sum(
                jnp.where(column < other_row, 1.0, 0.0), axis=0, keepdims=True
            )
    rows_out = jnp.concatenate(counts + [jnp.zeros((8 - len(counts), LANES), F32)], axis=0)
    table[...] = rows_out.astype(jnp.int32)


def project_kernel(
    wanted, store_slot, tokens, gain, middles, place, query_matrix, key_matrix, value_matrix, up, out
):
    total_rows = tokens.shape[0]
    first_home = lax.axis_index("ctx") * 2
    scaled = (tokens[...].astype(F32) * gain[...].astype(F32)).astype(BF16)
    packed = middles[...].astype(F32)
    lanes = lane_iota((total_rows, LANES))
    inverse = jnp.sum(
        jnp.where((lanes >= RANK) & (lanes < RANK + 3), packed, 0.0), axis=1, keepdims=True
    )
    place_column = jnp.concatenate(
        [column_of(place[part : part + 1, :]) for part in range(place.shape[0])], axis=0
    )
    use_first = jnp.zeros((total_rows, LANES), jnp.bool_)
    use_second = jnp.zeros((total_rows, LANES), jnp.bool_)
    for wanted_index in range(NEED):
        home = store_slot[wanted[wanted_index]]
        here = place_column == float(wanted_index)
        use_first = use_first | (here & (home == first_home))
        use_second = use_second | (here & (home == first_home + 1))
    spread = jnp.where(
        lanes < RANK,
        jnp.where(use_first, packed, 0.0),
        jnp.where(use_second, pltpu.roll(packed, RANK, 1), 0.0),
    ).astype(BF16)
    query_columns = query_matrix.shape[1]
    change = jnp.dot(spread, up[...], preferred_element_type=F32)
    query = jnp.dot(scaled, query_matrix[...], preferred_element_type=F32)
    out[:, :query_columns] = (query * inverse + ADAPTER_SCALE * change).astype(BF16)
    key = jnp.dot(scaled, key_matrix[...], preferred_element_type=F32)
    out[:, query_columns : query_columns + LANES] = (key * inverse).astype(BF16)
    value = jnp.dot(scaled, value_matrix[...], preferred_element_type=F32)
    out[:, query_columns + LANES :] = (value * inverse).astype(BF16)


def sum_kernel(parts, out):
    total = parts[0].astype(F32)
    for source in range(1, parts.shape[0]):
        total = total + parts[source].astype(F32)
    total = total.astype(BF16)
    for target in range(out.shape[0]):
        out[target] = total


def attention_kernel(table, vectors, keys, values, out, queries, peaks, masses, sums, scores):
    total_rows = vectors.shape[0]
    own_rows = 8
    block_count = keys.shape[0] // SPAN
    head_columns = GROUP * HEAD_WIDTH
    tall = GROUP * WINDOW
    window_row = row_iota((tall, LANES))
    window_row = window_row - WINDOW * (window_row // WINDOW)

    for g in range(GROUP):
        queries[g] = vectors[:, g * HEAD_WIDTH : (g + 1) * HEAD_WIDTH].astype(F32)
    peaks[...] = jnp.full(peaks.shape, LOWEST, F32)
    masses[...] = jnp.zeros(masses.shape, F32)
    sums[...] = jnp.zeros(sums.shape, F32)

    def window_of(block):
        begin = table[0, block]
        start = jnp.minimum((begin // 8) * 8, total_rows - WINDOW)
        return pl.multiple_of(start, 8), begin, table[1, block]

    def load(ref, start, length):
        return jnp.concatenate([ref[g, pl.ds(start, length), :] for g in range(GROUP)], axis=0)

    own_first = pl.multiple_of(lax.axis_index("ctx") * own_rows, own_rows)
    own_shape = (GROUP * own_rows, total_rows)
    own_row = row_iota(own_shape)
    own_row = own_row - own_rows * (own_row // own_rows)
    key_position = lane_iota(own_shape)
    fellow = jnp.zeros(own_shape, jnp.int32)
    for j in range(own_rows):
        position = own_first + j
        fellow = jnp.where(own_row == j, table[2 + position // LANES, position % LANES], fellow)
    own_allowed = (key_position >= fellow) & (key_position <= own_row + own_first)
    new_keys = vectors[:, head_columns : head_columns + HEAD_WIDTH]
    new_values = vectors[:, head_columns + HEAD_WIDTH :]
    own_queries = load(queries, own_first, own_rows).astype(BF16)
    own_scores = jnp.where(own_allowed, contract_last(own_queries, new_keys) * SCORE_SCALE, LOWEST)
    own_peak = own_scores[:, :LANES]
    for part in range(1, total_rows // LANES):
        own_peak = jnp.maximum(own_peak, own_scores[:, part * LANES : (part + 1) * LANES])
    for g in range(GROUP):
        peaks[g, pl.ds(own_first, own_rows), :] = own_peak[g * own_rows : (g + 1) * own_rows]

    unroll = 8

    def score_step(step, carry):
        found = []
        for k in range(unroll):
            block = step * unroll + k
            start, begin, end = window_of(block)
            key_block = keys[pl.ds(pl.multiple_of(block * SPAN, SPAN), SPAN), :]
            result = contract_last(load(queries, start, WINDOW).astype(BF16), key_block)
            position = window_row + start
            allowed = (position >= begin) & (position < end)
            result = jnp.where(allowed, result * SCORE_SCALE, LOWEST)
            scores[block] = result
            found.append((start, result))
        for start, result in found:
            for g in range(GROUP):
                place = pl.ds(start, WINDOW)
                peaks[g, place, :] = jnp.maximum(
                    peaks[g, place, :], result[g * WINDOW : (g + 1) * WINDOW]
                )
        return carry

    lax.fori_loop(0, block_count // unroll, score_step, 0)
    for g in range(GROUP):
        highest = jnp.max(peaks[g], axis=1, keepdims=True)
        peaks[g] = jnp.broadcast_to(jnp.maximum(highest, FLOOR), (total_rows, LANES))

    own_highest = load(peaks, own_first, own_rows)
    own_weights = jnp.concatenate(
        [
            jnp.exp2(own_scores[:, part * LANES : (part + 1) * LANES] - own_highest)
            for part in range(total_rows // LANES)
        ],
        axis=1,
    )
    own_mass = own_weights[:, :LANES]
    for part in range(1, total_rows // LANES):
        own_mass = own_mass + own_weights[:, part * LANES : (part + 1) * LANES]
    own_sum = jnp.dot(own_weights.astype(BF16), new_values, preferred_element_type=F32)
    for g in range(GROUP):
        masses[g, pl.ds(own_first, own_rows), :] = own_mass[g * own_rows : (g + 1) * own_rows]
        sums[g, pl.ds(own_first, own_rows), :] = own_sum[g * own_rows : (g + 1) * own_rows]

    def value_step(step, carry):
        found = []
        for k in range(unroll):
            block = step * unroll + k
            start, begin, end = window_of(block)
            weights = jnp.exp2(scores[block] - load(peaks, start, WINDOW))
            value_block = values[pl.ds(pl.multiple_of(block * SPAN, SPAN), SPAN), :]
            product = jnp.dot(weights.astype(BF16), value_block, preferred_element_type=F32)
            found.append((start, weights, product))
        for start, weights, product in found:
            for g in range(GROUP):
                place = pl.ds(start, WINDOW)
                rows = slice(g * WINDOW, (g + 1) * WINDOW)
                masses[g, place, :] = masses[g, place, :] + weights[rows]
                sums[g, place, :] = sums[g, place, :] + product[rows]
        return carry

    lax.fori_loop(0, block_count // unroll, value_step, 0)

    lanes = lane_iota((total_rows, LANES))
    quarter = lanes % GROUP
    peak_all = jnp.zeros((total_rows, LANES), F32)
    mass_all = jnp.zeros((total_rows, LANES), F32)
    for g in range(GROUP):
        mass = jnp.sum(masses[g], axis=1, keepdims=True)
        scale = jnp.where(mass > 0.0, 1.0 / mass, 0.0)
        out[:, g * HEAD_WIDTH : (g + 1) * HEAD_WIDTH] = (sums[g] * scale).astype(BF16)
        peak_all = jnp.where(quarter == g, peaks[g], peak_all)
        mass_all = jnp.where(quarter == g, mass, mass_all)
    notes = jnp.zeros((total_rows, LANES), F32)
    for index, part in enumerate(thirds(peak_all) + thirds(mass_all)):
        inside = (lanes >= GROUP * index) & (lanes < GROUP * (index + 1))
        notes = jnp.where(inside, part, notes)
    out[:, head_columns:] = notes.astype(BF16)


def combine_kernel(parts, out):
    sources, own_rows, _ = parts.shape
    head_columns = GROUP * HEAD_WIDTH
    peaks = []
    masses = []
    for source in range(sources):
        notes = parts[source, :, head_columns:].astype(F32)

        def from_lane(index):
            if index == 0:
                return notes
            return pltpu.roll(notes, LANES - GROUP * index, 1)

        peaks.append(from_lane(0) + from_lane(1) + from_lane(2))
        masses.append(from_lane(3) + from_lane(4) + from_lane(5))
    highest = peaks[0]
    for source in range(1, sources):
        highest = jnp.maximum(highest, peaks[source])
    weights = [masses[s] * jnp.exp2(peaks[s] - highest) for s in range(sources)]
    total = weights[0]
    for source in range(1, sources):
        total = total + weights[source]
    results = [jnp.zeros((own_rows, HEAD_WIDTH), F32) for _ in range(GROUP)]
    for source in range(sources):
        share = weights[source] / total
        for g in range(GROUP):
            part = parts[source, :, g * HEAD_WIDTH : (g + 1) * HEAD_WIDTH].astype(F32)
            results[g] = results[g] + share[:, g : g + 1] * part
    block = jnp.concatenate(results, axis=1).astype(BF16)
    for target in range(out.shape[0]):
        out[target] = block


def shards(
    tokens,
    input_norm_gain,
    query_matrix,
    key_matrix,
    value_matrix,
    output_matrix,
    cached_key_rows,
    cached_value_rows,
    cache_block_recording,
    stretch_token_recording,
    adapter_down_store,
    adapter_up_store,
    adapter_store_slot,
    adapter_wanted_list,
    token_adapter_place,
):
    total_rows = tokens.shape[0]
    ctx_count = lax.axis_size("ctx")
    head_count = lax.axis_size("head")
    own_rows = total_rows // ctx_count
    head_rows = total_rows // head_count
    query_columns = query_matrix.shape[1]
    all_columns = query_columns + 2 * HEAD_WIDTH
    gain = input_norm_gain.reshape(1, LANES)
    place = token_adapter_place.reshape(total_rows // LANES, LANES)
    stretch = stretch_token_recording.reshape(total_rows // LANES, LANES)
    cache = jnp.pad(cache_block_recording, (0, LANES - cache_block_recording.shape[0])).reshape(1, LANES)
    down = adapter_down_store.reshape(2 * RANK, MODEL_WIDTH)
    up = adapter_up_store.reshape(2 * RANK, query_columns)

    packed = call(
        pack_tokens,
        jax.ShapeDtypeStruct((ctx_count, head_rows + 8, LANES), BF16),
        [VMEM, VMEM],
        name="pack_tokens",
    )(tokens, gain)
    blocks = lax.all_to_all(packed, "ctx", 0, 0, tiled=True)
    middles, table = call(
        middle_kernel,
        (
            jax.ShapeDtypeStruct((head_count, head_rows, LANES), BF16),
            jax.ShapeDtypeStruct((8, LANES), jnp.int32),
        ),
        [SMEM, SMEM] + [VMEM] * 5,
        [pltpu.VMEM((head_rows, MODEL_WIDTH), BF16), pltpu.VMEM((total_rows, LANES), F32)],
        name="adapter_middle",
    )(adapter_wanted_list, adapter_store_slot, blocks, down, place, stretch, cache)
    middles = lax.all_to_all(middles, "head", 0, 0, tiled=True).reshape(total_rows, LANES)
    partial = call(
        project_kernel,
        jax.ShapeDtypeStruct((total_rows, all_columns), BF16),
        [SMEM, SMEM] + [VMEM] * 8,
        name="project",
    )(
        adapter_wanted_list,
        adapter_store_slot,
        tokens,
        gain,
        middles,
        place,
        query_matrix,
        key_matrix,
        value_matrix,
        up,
    )
    partial = lax.all_to_all(
        partial.reshape(ctx_count, own_rows, all_columns), "ctx", 0, 0, tiled=True
    )
    vectors = call(
        sum_kernel,
        jax.ShapeDtypeStruct((ctx_count, own_rows, all_columns), BF16),
        [VMEM],
        name="sum_projections",
    )(partial)
    vectors = lax.all_to_all(vectors, "ctx", 0, 0, tiled=True).reshape(total_rows, all_columns)
    block_count = cached_key_rows.shape[0] // SPAN
    state = pltpu.VMEM((GROUP, total_rows, LANES), F32)
    parts = call(
        attention_kernel,
        jax.ShapeDtypeStruct((total_rows, query_columns + LANES), BF16),
        [SMEM] + [VMEM] * 3,
        [state, state, state, state, pltpu.VMEM((block_count, GROUP * WINDOW, LANES), F32)],
        limit=24,
        name="attention",
    )(table, vectors, cached_key_rows, cached_value_rows)
    parts = lax.all_to_all(
        parts.reshape(ctx_count, own_rows, query_columns + LANES), "ctx", 0, 0, tiled=True
    )
    attention = call(
        combine_kernel,
        jax.ShapeDtypeStruct((ctx_count, own_rows, query_columns), BF16),
        [VMEM],
        name="combine",
    )(parts)
    attention = lax.all_to_all(attention, "ctx", 0, 0, tiled=True).reshape(total_rows, query_columns)
    mixed = jnp.dot(attention, output_matrix, preferred_element_type=F32)
    mixed = lax.all_to_all(mixed.reshape(head_count, head_rows, LANES), "head", 0, 0, tiled=True)
    return jnp.sum(mixed, axis=0).astype(BF16)


def solution(mesh):
    in_specs = (
        P(None, "ctx"),
        P("ctx"),
        P("ctx", "head"),
        P("ctx", "head"),
        P("ctx", "head"),
        P("head", "ctx"),
        P("ctx", "head"),
        P("ctx", "head"),
        P("ctx"),
        P(),
        P("ctx", None, None),
        P("ctx", None, "head"),
        P(),
        P(),
        P(),
    )
    out_specs = P("head", "ctx")
    return jax.shard_map(shards, mesh=mesh, in_specs=in_specs, out_specs=out_specs, check_vma=False)
```

time: 743 us -> 131 us (0.18)
  waiting for transfers between devices: 343 us -> 9.52 us
  loops' own time: 85 us -> 0 us
  local copies, waits for them, and re-layouts: 76.4 us -> 6.13 us
  other arithmetic: 54.3 us -> 0.61 us
  blocking collectives: 129 us -> 92.3 us
  matrix products: 25.7 us -> 0.21 us
  between operations: 24.4 us -> 0.11 us
  starting transfers between devices: 0.13 us -> 11.9 us
  Pallas kernels: 0 us -> 9.41 us
    psum x2 -> x0, waiting for transfers between devices: 239 us -> none  [the longest x1 153 us: spread(): return lax.psum(block, axis)]
    all_to_all x0 -> x6, blocking collectives: none -> 92.3 us  [the longest x1 18.3 us: shards(): lax.all_to_all(vectors, 'ctx', 0, 0, tiled=True)]
    another operation x34 -> x0, loops' own time: 85 us -> none  [the longest x1 82.8 us: shards(): lax.scan(cache_step, carried, (key_blocks, value_blocks, record_blocks))]
    all_gather x1 -> x0, waiting for transfers between devices: 76.1 us -> none  [joined(): gathered = jax.tree.map(lambda a: lax.all_gather(a, axis), part)]
    all_gather x2 -> x0, blocking collectives: 70.8 us -> none  [joined(): gathered = jax.tree.map(lambda a: lax.all_gather(a, axis), part)]
    psum x1 -> x0, blocking collectives: 58.2 us -> none  [shards(): lax.psum((query_part, middle_product, squares), 'ctx')]
    add x79 -> x0, other arithmetic: 43.9 us -> none  [the longest x31 42.8 us: join_states(): first_state[2].reshape(total_rows, head_count, HEAD_WIDTH)]
    reduce_scatter x1 -> x0, waiting for transfers between devices: 27.9 us -> none  [shards(): lax.psum_scatter(jnp.dot(attention, output_matrix, preferred_element_type...]
  transfers between devices with their start and end apart: 4 -> 1, of which waited for: 4 -> 1; matrix products, arithmetic and copies ran while one was open for 1% -> 1% of each run, Pallas kernels for 0% -> 0%
where the time goes in v1:
time: 131 us; the launch traced here: 130 us
  blocking collectives  92.3 us (70%)
  starting transfers between devices  11.9 us (9%)
  waiting for transfers between devices  9.52 us (7%)
  Pallas kernels  9.41 us (7%)
  local copies, waits for them, and re-layouts  6.13 us (5%)
    all_to_all x1, blocking collectives, shards(): lax.all_to_all(vectors, 'ctx', 0, 0, tiled=True)  18.3 us
    all_to_all x1, blocking collectives, shards(): lax.all_to_all(parts.reshape(ctx_count, own_rows, query_columns + LANES),...  17.3 us
    all_to_all x1, blocking collectives, shards(): lax.all_to_all(attention, 'ctx', 0, 0, tiled=True)  15.6 us
    all_to_all x1, blocking collectives, shards(): lax.all_to_all(partial.reshape(ctx_count, own_rows, all_columns), 'ctx',...  15.5 us
    all_to_all x1, blocking collectives, shards(): lax.all_to_all(middles, 'head', 0, 0, tiled=True).reshape(total_rows, LANES)  13.6 us
    all_to_all x1, blocking collectives, shards(): lax.all_to_all(mixed.reshape(head_count, head_rows, LANES), 'head', 0, 0,...  12.1 us
    all_to_all x1, starting transfers between devices, shards(): blocks = lax.all_to_all(packed, 'ctx', 0, 0, tiled=True)  11.9 us
    all_to_all x1, waiting for transfers between devices, shards(): blocks = lax.all_to_all(packed, 'ctx', 0, 0, tiled=True)  9.52 us
  transfers between devices with their start and end apart: 1, of which 1 were waited for; matrix products, arithmetic and copies ran while one was open for 1% of the time, Pallas kernels for 0%

profile of v1, /device:TPU:1, one launch (start us, length us, event | category | flops | bytes accessed | tf_op | source)
XLA Modules:
  0.0 130.2 jit_solution(16908217923496875969)
XLA Ops:
  0.0 0.9 copy-done.4
  0.9 0.7 copy-done.13
  1.6 0.8 pack_tokens.1
  2.3 11.9 %all-to-all-start = ((bf16[32,40,128]{2,1,0:T(8,128)(2,1)}), bf16[32,40,128]{2,1,0:T(8,128)(2,1)S(1)}, u32[]{:S(2)}, u32[]{:S(2)}) async-start(bf16[32,40,128]{2,1,0:T(8,128)(2,1)} %pack_tokens.1), calls=%async_computation | async-start | bytes 655360 | tf_op jit(solution)/shard_map/all_to_all | solution.py:366
  14.2 0.7 pad_bitcast_fusion.cache
  14.9 9.5 %all-to-all-done.blocks = bf16[32,40,128]{2,1,0:T(8,128)(2,1)S(1)} async-done(((bf16[32,40,128]{2,1,0:T(8,128)(2,1)}), bf16[32,40,128]{2,1,0:T(8,128)(2,1)S(1)}, u32[]{:S(2)}, u32[]{:S(2)}) %all-to-all-start) | async-done | bytes 327712 | tf_op jit(solution)/shard_map/all_to_all | solution.py:366
  24.4 1.2 copy-done.3
  25.6 0.7 copy-done.10
  26.3 0.7 copy-done.11
  27.0 0.7 copy-done.12
  27.6 0.7 copy-done.15
  28.3 1.1 adapter_middle.1
  29.4 13.6 %all_to_all.35 = bf16[8,32,128]{2,1,0:T(8,128)(2,1)S(1)} all-to-all(bf16[8,32,128]{2,1,0:T(8,128)(2,1)S(1)} %get-tuple-element.8), channel_id=1, replica_groups=mesh['ctx'=32,'head'=8] {'head'}, dimensions={0} | all-to-all | bytes 131072 | tf_op jit(solution)/shard_map/all_to_all | solution.py:377
  43.1 1.1 project.1
  44.2 15.5 %all_to_all.36.parts = bf16[32,8,768]{2,1,0:T(8,128)(2,1)S(1)} all-to-all(bf16[32,8,768]{2,1,0:T(8,128)(2,1)S(1)} %bitcast.16), channel_id=1, replica_groups=mesh['ctx'=32,'head'=8] {'ctx'}, dimensions={0} | all-to-all | bytes 786432 | tf_op jit(solution)/shard_map/all_to_all | solution.py:395
  59.7 0.1 sum_projections.1
  59.8 18.3 %all_to_all.37 = bf16[32,8,768]{2,1,0:T(8,128)(2,1)S(1)} all-to-all(bf16[32,8,768]{2,1,0:T(8,128)(2,1)S(1)} %sum_projections.1), channel_id=1, replica_groups=mesh['ctx'=32,'head'=8] {'ctx'}, dimensions={0} | all-to-all | bytes 786432 | tf_op jit(solution)/shard_map/all_to_all | solution.py:404
  78.1 5.8 %attention.1 = bf16[256,640]{1,0:T(8,128)(2,1)S(1)} custom-call(s32[8,128]{1,0:T(8,128)S(1)} %get-tuple-element.7.table, bf16[256,768]{1,0:T(8,128)(2,1)S(1)} %bitcast.17, bf16[8192,128]{1,0:T(8,128)(2,1)S(1)} %copy-done.1, bf16[8192,128]{1,0:T(8,128)(2,1)S(1)} %copy-done.2), custom_call_target="tpu_custom_call" | custom-call | tf_op jit(solution)/shard_map/attention/pallas_call | solution.py:407
  83.9 17.3 %all_to_all.38.parts = bf16[32,8,640]{2,1,0:T(8,128)(2,1)S(1)} all-to-all(bf16[32,8,640]{2,1,0:T(8,128)(2,1)S(1)} %bitcast.18), channel_id=1, replica_groups=mesh['ctx'=32,'head'=8] {'ctx'}, dimensions={0} | all-to-all | bytes 655360 | tf_op jit(solution)/shard_map/all_to_all | solution.py:415
  101.1 0.5 combine.1
  101.6 15.6 %all_to_all.39 = bf16[32,8,512]{2,1,0:T(8,128)(2,1)S(1)} all-to-all(bf16[32,8,512]{2,1,0:T(8,128)(2,1)S(1)} %combine.1), channel_id=1, replica_groups=mesh['ctx'=32,'head'=8] {'ctx'}, dimensions={0} | all-to-all | bytes 524288 | tf_op jit(solution)/shard_map/all_to_all | solution.py:424
  117.3 0.2 fusion
  117.5 12.1 %all_to_all.40 = f32[8,32,128]{2,1,0:T(8,128)S(1)} all-to-all(f32[8,32,128]{2,1,0:T(8,128)S(1)} %fusion), channel_id=1, replica_groups=mesh['ctx'=32,'head'=8] {'head'}, dimensions={0} | all-to-all | bytes 262144 | tf_op jit(solution)/shard_map/all_to_all | solution.py:426
  129.5 0.6 reduce_sum.9
  (25 shorter events, 0.0 us)
Async XLA Ops:
  0.0 117.3 %copy-start = (bf16[512,128]{1,0:T(8,128)(2,1)S(1)}, bf16[512,128]{1,0:T(8,128)(2,1)}, u32[]{:S(2)}) copy-start(bf16[512,128]{1,0:T(8,128)(2,1)} %param.20) | copy-start | bytes 393220
  0.0 43.0 %copy-start.14 = (bf16[128]{0:T(256)(128)(2,1)S(1)}, bf16[128]{0:T(256)(128)(2,1)}, u32[]{:S(2)}) copy-start(bf16[128]{0:T(256)(128)(2,1)} %param.16) | copy-start | bytes 772
  0.0 0.9 copy-start.4
  0.9 0.7 copy-start.13
  1.6 41.5 %copy-start.5 = (bf16[256,128]{1,0:T(8,128)(2,1)S(1)}, bf16[256,128]{1,0:T(8,128)(2,1)}, u32[]{:S(2)}) copy-start(bf16[256,128]{1,0:T(8,128)(2,1)} %tokens.3) | copy-start | bytes 196612
  1.6 41.5 %copy-start.6 = (bf16[128,512]{1,0:T(8,128)(2,1)S(1)}, bf16[128,512]{1,0:T(8,128)(2,1)}, u32[]{:S(2)}) copy-start(bf16[128,512]{1,0:T(8,128)(2,1)} %query_matrix.1) | copy-start | bytes 393220
  1.6 41.5 %copy-start.7 = (bf16[2,64,512]{2,1,0:T(8,128)(2,1)S(1)}, bf16[2,64,512]{2,1,0:T(8,128)(2,1)}, u32[]{:S(2)}) copy-start(bf16[2,64,512]{2,1,0:T(8,128)(2,1)} %param.26) | copy-start | bytes 393220
  1.6 41.5 %copy-start.8 = (bf16[128,128]{1,0:T(8,128)(2,1)S(1)}, bf16[128,128]{1,0:T(8,128)(2,1)}, u32[]{:S(2)}) copy-start(bf16[128,128]{1,0:T(8,128)(2,1)} %key_matrix.1) | copy-start | bytes 98308
  1.6 41.5 %copy-start.9 = (bf16[128,128]{1,0:T(8,128)(2,1)S(1)}, bf16[128,128]{1,0:T(8,128)(2,1)}, u32[]{:S(2)}) copy-start(bf16[128,128]{1,0:T(8,128)(2,1)} %value_matrix.1) | copy-start | bytes 98308
  2.3 22.1 %all-to-all-start = ((bf16[32,40,128]{2,1,0:T(8,128)(2,1)}), bf16[32,40,128]{2,1,0:T(8,128)(2,1)S(1)}, u32[]{:S(2)}, u32[]{:S(2)}) async-start(bf16[32,40,128]{2,1,0:T(8,128)(2,1)} %pack_tokens.1), calls=%async_computation | async-start | bytes 655360 | tf_op jit(solution)/shard_map/all_to_all | solution.py:366
  24.4 1.2 copy-start.3
  25.6 0.7 copy-start.10
  26.3 0.7 copy-start.11
  27.0 0.7 copy-start.12
  27.6 0.7 copy-start.15
  28.3 49.8 %copy-start.1 = (bf16[8192,128]{1,0:T(8,128)(2,1)S(1)}, bf16[8192,128]{1,0:T(8,128)(2,1)}, u32[]{:S(2)}) copy-start(bf16[8192,128]{1,0:T(8,128)(2,1)} %keys.1) | copy-start | bytes 6291460
  28.3 49.8 %copy-start.2 = (bf16[8192,128]{1,0:T(8,128)(2,1)S(1)}, bf16[8192,128]{1,0:T(8,128)(2,1)}, u32[]{:S(2)}) copy-start(bf16[8192,128]{1,0:T(8,128)(2,1)} %values.1) | copy-start | bytes 6291460

commit v2 on v1

v2 whole, which is shorter than its diff:
```python
import math

import jax
import jax.numpy as jnp
from jax import lax
from jax.experimental import pallas as pl
from jax.experimental.pallas import tpu as pltpu
from jax.sharding import PartitionSpec as P

MODEL_WIDTH = 4096
HEAD_WIDTH = 128
LANES = 128
SPAN = 128
NEED = 4
GROUP = 4
RANK = 64
WINDOW = 24

LOWEST = -1e30
FLOOR = -1e29
EPSILON = 1e-05
ADAPTER_SCALE = 0.5
SCORE_SCALE = math.log2(math.e) / math.sqrt(HEAD_WIDTH)

F32 = jnp.float32
BF16 = jnp.bfloat16
VMEM = pl.BlockSpec(memory_space=pltpu.VMEM)
SMEM = pl.BlockSpec(memory_space=pltpu.SMEM)
HBM = pl.BlockSpec(memory_space=pltpu.HBM)


def lane_iota(shape):
    return lax.broadcasted_iota(jnp.int32, shape, len(shape) - 1)


def row_iota(shape):
    return lax.broadcasted_iota(jnp.int32, shape, len(shape) - 2)


def column_of(row):
    return jnp.transpose(jnp.broadcast_to(row.astype(F32), (LANES, LANES)))


def thirds(value):
    high = value.astype(BF16).astype(F32)
    rest = value - high
    middle = rest.astype(BF16).astype(F32)
    return high, middle, rest - middle


def contract_last(a, b):
    return lax.dot_general(a, b, (((1,), (1,)), ((), ())), preferred_element_type=F32)


def call(body, out_shape, in_specs, scratch=(), limit=16, flops=0, name=None):
    many = isinstance(out_shape, (tuple, list))
    return pl.pallas_call(
        body,
        out_shape=out_shape,
        in_specs=in_specs,
        out_specs=[VMEM] * len(out_shape) if many else VMEM,
        scratch_shapes=list(scratch),
        compiler_params=pltpu.CompilerParams(vmem_limit_bytes=limit * 1024 * 1024),
        name=name,
    )


SLOT_ROW, WANTED_ROW = 0, 1


def home_of(numbers, wanted_index):
    return numbers[SLOT_ROW, numbers[WANTED_ROW, wanted_index]]


def pack_kernel(tokens_hbm, gain_hbm, out, tokens, gain, arrived):
    rows = tokens.shape[0]
    first = pl.multiple_of(lax.axis_index("head") * rows, rows)
    copies = [
        pltpu.make_async_copy(tokens_hbm.at[pl.ds(first, rows), :], tokens, arrived.at[0]),
        pltpu.make_async_copy(gain_hbm, gain, arrived.at[1]),
    ]
    for copy in copies:
        copy.start()
    for copy in copies:
        copy.wait()
    gain_rows = jnp.broadcast_to(gain[...].astype(F32), (8, LANES))
    block = jnp.concatenate([tokens[...].astype(F32), gain_rows], axis=0).astype(BF16)
    for target in range(out.shape[0]):
        out[target] = block


def early_kernel(
    place,
    stretch,
    cache,
    slot,
    wanted,
    down_hbm,
    numbers,
    ranges,
    places,
    down,
    arrived,
):
    copy = pltpu.make_async_copy(down_hbm, down, arrived)
    copy.start()
    numbers[...] = jnp.zeros(numbers.shape, jnp.int32)
    for row, part in ((SLOT_ROW, slot), (WANTED_ROW, wanted)):
        numbers[row : row + 1, : part.shape[1]] = part[...]
    parts = place.shape[0]
    for part in range(parts):
        places[part * LANES : (part + 1) * LANES, :] = column_of(place[part : part + 1, :])

    def wide(row):
        return jnp.broadcast_to(row.astype(F32), (LANES, LANES))

    cache_row = jnp.concatenate(
        [cache[...], jnp.zeros((1, LANES - cache.shape[1]), jnp.int32)], axis=1
    )
    uppers = [cache_row] + [stretch[part : part + 1, :] for part in range(parts)]
    counts = [jnp.zeros((1, LANES), F32) for _ in range(1 + len(uppers))]
    for part in range(parts):
        column = column_of(stretch[part : part + 1, :])
        below = jnp.where(column < wide(cache_row), 1.0, 0.0)
        counts[0] = counts[0] + jnp.sum(below, axis=0, keepdims=True)
        for index, row in enumerate(uppers):
            below = jnp.where(column <= wide(row), 1.0, 0.0)
            counts[1 + index] = counts[1 + index] + jnp.sum(below, axis=0, keepdims=True)
    counts.append(jnp.zeros((8 - len(counts), LANES), F32))
    ranges[...] = jnp.concatenate(counts, axis=0).astype(jnp.int32)
    copy.wait()


def adapter_choice(numbers, place, first_home):
    use_first = jnp.zeros(place.shape, jnp.bool_)
    use_second = jnp.zeros(place.shape, jnp.bool_)
    for wanted_index in range(NEED):
        home = home_of(numbers, wanted_index)
        here = place == float(wanted_index)
        use_first = use_first | (here & (home == first_home))
        use_second = use_second | (here & (home == first_home + 1))
    return use_first, use_second


def middle_kernel(numbers, places, blocks, down, out, flat):
    rows = flat.shape[0]
    squares = jnp.zeros((rows, LANES), F32)
    for source in range(blocks.shape[0]):
        block = blocks[source].astype(F32)
        token_part = block[:rows]
        squares = squares + token_part * token_part
        scaled = (token_part * block[rows : rows + 1]).astype(BF16)
        flat[:, source * LANES : (source + 1) * LANES] = scaled
    mean = jnp.sum(squares, axis=1, keepdims=True) / MODEL_WIDTH
    inverse = lax.rsqrt(mean + EPSILON)
    middle = contract_last(flat[...], down[...]) * inverse
    first = pl.multiple_of(lax.axis_index("head") * rows, rows)
    use_first, use_second = adapter_choice(
        numbers, places[pl.ds(first, rows), :], lax.axis_index("ctx") * 2
    )
    picked = jnp.where(
        use_first, middle, jnp.where(use_second, pltpu.roll(middle, RANK, 1), 0.0)
    )
    picked = picked.astype(BF16).astype(F32)
    packed = jnp.where(
        lane_iota((rows, LANES)) < RANK, picked, jnp.broadcast_to(inverse, (rows, LANES))
    )
    for target in range(out.shape[0]):
        out[target] = packed


def project_kernel(
    numbers, places, tokens, gain, middles, query_matrix, key_matrix, value_matrix, up, out
):
    scaled = (tokens[...].astype(F32) * gain[...].astype(F32)).astype(BF16)
    packed = middles[...]
    lanes = lane_iota(packed.shape)
    inverse = packed[:, RANK : RANK + 1]
    use_first, use_second = adapter_choice(numbers, places[...], lax.axis_index("ctx") * 2)
    spread = jnp.where(
        lanes < RANK,
        jnp.where(use_first, packed, 0.0),
        jnp.where(use_second, pltpu.roll(packed, RANK, 1), 0.0),
    ).astype(BF16)
    columns = up.shape[1]
    change = jnp.dot(spread, up[...], preferred_element_type=F32)
    query = jnp.dot(scaled, query_matrix[...], preferred_element_type=F32)
    out[:, :columns] = (query * inverse + ADAPTER_SCALE * change).astype(BF16)
    key = jnp.dot(scaled, key_matrix[...], preferred_element_type=F32)
    out[:, columns : columns + HEAD_WIDTH] = (key * inverse).astype(BF16)
    value = jnp.dot(scaled, value_matrix[...], preferred_element_type=F32)
    out[:, columns + HEAD_WIDTH :] = (value * inverse).astype(BF16)


def sum_kernel(parts, out, own_pair):
    total = parts[0].astype(F32)
    for source in range(1, parts.shape[0]):
        total = total + parts[source].astype(F32)
    query_columns = out.shape[2]
    queries = total[:, :query_columns].astype(BF16)
    for target in range(out.shape[0]):
        out[target] = queries
    own_pair[...] = total[:, query_columns:]


def attention_kernel(
    ranges,
    vectors,
    own_pair,
    keys,
    values,
    out,
    queries,
    peaks,
    masses,
    sums,
    scores,
):
    sources, own_rows, _ = vectors.shape
    total_rows = sources * own_rows
    block_count = keys.shape[0] // SPAN
    head_columns = GROUP * HEAD_WIDTH
    tall = GROUP * WINDOW
    window_row = row_iota((tall, LANES))
    window_row = window_row - WINDOW * (window_row // WINDOW)
    peaks[...] = jnp.full(peaks.shape, LOWEST, F32)
    masses[...] = jnp.zeros(masses.shape, F32)
    sums[...] = jnp.zeros(sums.shape, F32)

    lanes = lane_iota((total_rows, LANES))
    for g in range(GROUP):
        for source in range(sources):
            queries[g, source * own_rows : (source + 1) * own_rows, :] = vectors[
                source, :, g * HEAD_WIDTH : (g + 1) * HEAD_WIDTH
            ].astype(F32)

    def window_of(block):
        begin = ranges[0, block]
        start = jnp.minimum((begin // 8) * 8, total_rows - WINDOW)
        return pl.multiple_of(start, 8), begin, ranges[1, block]

    def load(ref, start):
        return jnp.concatenate([ref[g, pl.ds(start, WINDOW), :] for g in range(GROUP)], axis=0)

    def raise_peaks(start, result):
        for g in range(GROUP):
            place = pl.ds(start, WINDOW)
            peaks[g, place, :] = jnp.maximum(
                peaks[g, place, :], result[g * WINDOW : (g + 1) * WINDOW]
            )

    def add_up(start, weights, product):
        for g in range(GROUP):
            place = pl.ds(start, WINDOW)
            rows = slice(g * WINDOW, (g + 1) * WINDOW)
            masses[g, place, :] = masses[g, place, :] + weights[rows]
            sums[g, place, :] = sums[g, place, :] + product[rows]

    own_first = pl.multiple_of(lax.axis_index("ctx") * own_rows, own_rows)
    padding = jnp.zeros((LANES - own_rows, HEAD_WIDTH), F32)
    new_keys = jnp.concatenate([own_pair[:, :HEAD_WIDTH], padding], axis=0).astype(BF16)
    new_values = jnp.concatenate([own_pair[:, HEAD_WIDTH:], padding], axis=0).astype(BF16)
    own_start = pl.multiple_of(jnp.minimum(own_first, total_rows - WINDOW), 8)
    key_lane = lane_iota((tall, LANES))
    ends = jnp.zeros((tall, LANES), jnp.int32)
    for j in range(own_rows):
        position = own_first + j
        ends = jnp.where(key_lane == j, ranges[2 + position // LANES, position % LANES], ends)
    query_position = window_row + own_start
    allowed = (key_lane + own_first <= query_position) & (query_position < ends)
    own_scores = contract_last(load(queries, own_start).astype(BF16), new_keys)
    own_scores = jnp.where(allowed, own_scores * SCORE_SCALE, LOWEST)
    raise_peaks(own_start, own_scores)

    unroll = 32

    def score_step(step, carry):
        found = []
        for k in range(unroll):
            block = step * unroll + k
            start, begin, end = window_of(block)
            key_block = keys[pl.ds(pl.multiple_of(block * SPAN, SPAN), SPAN), :]
            result = contract_last(load(queries, start).astype(BF16), key_block)
            position = window_row + start
            allowed = (position >= begin) & (position < end)
            result = jnp.where(allowed, result * SCORE_SCALE, LOWEST)
            scores[block] = result
            found.append((start, result))
        for start, result in found:
            raise_peaks(start, result)
        return carry

    lax.fori_loop(0, block_count // unroll, score_step, 0)
    for g in range(GROUP):
        highest = jnp.max(peaks[g], axis=1, keepdims=True)
        peaks[g] = jnp.broadcast_to(jnp.maximum(highest, FLOOR), (total_rows, LANES))

    own_weights = jnp.exp2(own_scores - load(peaks, own_start))
    add_up(
        own_start,
        own_weights,
        jnp.dot(own_weights.astype(BF16), new_values, preferred_element_type=F32),
    )

    def value_step(step, carry):
        found = []
        for k in range(unroll):
            block = step * unroll + k
            start, begin, end = window_of(block)
            weights = jnp.exp2(scores[block] - load(peaks, start))
            value_block = values[pl.ds(pl.multiple_of(block * SPAN, SPAN), SPAN), :]
            product = jnp.dot(weights.astype(BF16), value_block, preferred_element_type=F32)
            found.append((start, weights, product))
        for start, weights, product in found:
            add_up(start, weights, product)
        return carry

    lax.fori_loop(0, block_count // unroll, value_step, 0)

    quarter = lanes % GROUP
    peak_all = jnp.zeros((total_rows, LANES), F32)
    mass_all = jnp.zeros((total_rows, LANES), F32)
    for g in range(GROUP):
        mass = jnp.sum(masses[g], axis=1, keepdims=True)
        scale = jnp.where(mass > 0.0, 1.0 / mass, 0.0)
        out[:, g * HEAD_WIDTH : (g + 1) * HEAD_WIDTH] = (sums[g] * scale).astype(BF16)
        peak_all = jnp.where(quarter == g, peaks[g], peak_all)
        mass_all = jnp.where(quarter == g, mass, mass_all)
    notes = jnp.zeros((total_rows, LANES), F32)
    for index, part in enumerate(thirds(peak_all) + thirds(mass_all)):
        inside = (lanes >= GROUP * index) & (lanes < GROUP * (index + 1))
        notes = jnp.where(inside, part, notes)
    out[:, head_columns:] = notes.astype(BF16)


def combine_kernel(parts, out):
    sources, own_rows, _ = parts.shape
    head_columns = GROUP * HEAD_WIDTH
    peaks = []
    masses = []
    for source in range(sources):
        notes = parts[source, :, head_columns:].astype(F32)

        def from_lane(index):
            if index == 0:
                return notes
            return pltpu.roll(notes, LANES - GROUP * index, 1)

        peaks.append(from_lane(0) + from_lane(1) + from_lane(2))
        masses.append(from_lane(3) + from_lane(4) + from_lane(5))
    highest = peaks[0]
    for source in range(1, sources):
        highest = jnp.maximum(highest, peaks[source])
    weights = [masses[s] * jnp.exp2(peaks[s] - highest) for s in range(sources)]
    total = weights[0]
    for source in range(1, sources):
        total = total + weights[source]
    results = [jnp.zeros((own_rows, HEAD_WIDTH), F32) for _ in range(GROUP)]
    for source in range(sources):
        share = weights[source] / total
        for g in range(GROUP):
            part = parts[source, :, g * HEAD_WIDTH : (g + 1) * HEAD_WIDTH].astype(F32)
            results[g] = results[g] + share[:, g : g + 1] * part
    block = jnp.concatenate(results, axis=1).astype(BF16)
    for target in range(out.shape[0]):
        out[target] = block


def shards(
    tokens,
    input_norm_gain,
    query_matrix,
    key_matrix,
    value_matrix,
    output_matrix,
    cached_key_rows,
    cached_value_rows,
    cache_block_recording,
    stretch_token_recording,
    adapter_down_store,
    adapter_up_store,
    adapter_store_slot,
    adapter_wanted_list,
    token_adapter_place,
):
    total_rows = tokens.shape[0]
    ctx_count = lax.axis_size("ctx")
    head_count = lax.axis_size("head")
    own_rows = total_rows // ctx_count
    head_rows = total_rows // head_count
    query_columns = query_matrix.shape[1]
    block_count = cached_key_rows.shape[0] // SPAN
    down = adapter_down_store.reshape(2 * RANK, MODEL_WIDTH)
    up = adapter_up_store.reshape(2 * RANK, query_columns)

    place = token_adapter_place.reshape(total_rows // LANES, LANES)
    stretch = stretch_token_recording.reshape(total_rows // LANES, LANES)
    cache = cache_block_recording.reshape(1, block_count)
    slot = adapter_store_slot.reshape(1, adapter_store_slot.shape[0])
    wanted = adapter_wanted_list.reshape(1, NEED)
    gain = input_norm_gain.reshape(1, LANES)
    packed = call(
        pack_kernel,
        jax.ShapeDtypeStruct((ctx_count, head_rows + 8, LANES), BF16),
        [HBM, HBM],
        [
            pltpu.VMEM((head_rows, LANES), BF16),
            pltpu.VMEM((1, LANES), BF16),
            pltpu.SemaphoreType.DMA((2,)),
        ],
        limit=60,
        name="pack_tokens",
    )(tokens, gain)
    blocks = lax.all_to_all(packed, "ctx", 0, 0, tiled=True)
    all_columns = query_columns + 2 * HEAD_WIDTH
    numbers, ranges, places, down = call(
        early_kernel,
        (
            jax.ShapeDtypeStruct((8, LANES), jnp.int32),
            jax.ShapeDtypeStruct((8, LANES), jnp.int32),
            jax.ShapeDtypeStruct((total_rows, LANES), F32),
            jax.ShapeDtypeStruct(down.shape, BF16),
        ),
        [VMEM] * 5 + [HBM],
        [pltpu.SemaphoreType.DMA],
        name="early",
    )(place, stretch, cache, slot, wanted, down)
    middles = call(
        middle_kernel,
        jax.ShapeDtypeStruct((head_count, head_rows, LANES), F32),
        [SMEM] + [VMEM] * 3,
        [pltpu.VMEM((head_rows, MODEL_WIDTH), BF16)],
        name="adapter_middle",
    )(numbers, places, blocks, down)
    middles = lax.all_to_all(middles, "head", 0, 0, tiled=True).reshape(total_rows, LANES)
    partial = call(
        project_kernel,
        jax.ShapeDtypeStruct((total_rows, all_columns), BF16),
        [SMEM] + [VMEM] * 8,
        name="project",
    )(
        numbers,
        places,
        tokens,
        gain,
        middles,
        query_matrix,
        key_matrix,
        value_matrix,
        up,
    )
    partial = lax.all_to_all(
        partial.reshape(ctx_count, own_rows, all_columns), "ctx", 0, 0, tiled=True
    )
    vectors, own_pair = call(
        sum_kernel,
        (
            jax.ShapeDtypeStruct((ctx_count, own_rows, query_columns), BF16),
            jax.ShapeDtypeStruct((own_rows, 2 * HEAD_WIDTH), F32),
        ),
        [VMEM],
        name="sum_projections",
    )(partial)
    vectors = lax.all_to_all(vectors, "ctx", 0, 0, tiled=True)
    state = pltpu.VMEM((GROUP, total_rows, LANES), F32)
    parts = call(
        attention_kernel,
        jax.ShapeDtypeStruct((total_rows, query_columns + LANES), BF16),
        [SMEM] + [VMEM] * 4,
        [
            state,
            state,
            state,
            state,
            pltpu.VMEM((block_count, GROUP * WINDOW, LANES), F32),
        ],
        limit=24,
        name="attention",
    )(ranges, vectors, own_pair, cached_key_rows, cached_value_rows)
    parts = lax.all_to_all(
        parts.reshape(ctx_count, own_rows, query_columns + LANES), "ctx", 0, 0, tiled=True
    )
    attention = call(
        combine_kernel,
        jax.ShapeDtypeStruct((ctx_count, own_rows, query_columns), BF16),
        [VMEM],
        name="combine",
    )(parts)
    attention = lax.all_to_all(attention, "ctx", 0, 0, tiled=True).reshape(total_rows, query_columns)
    mixed = jnp.dot(attention, output_matrix, preferred_element_type=F32)
    mixed = lax.all_to_all(mixed.reshape(head_count, head_rows, LANES), "head", 0, 0, tiled=True)
    return jnp.sum(mixed, axis=0).astype(BF16)


def solution(mesh):
    in_specs = (
        P(None, "ctx"),
        P("ctx"),
        P("ctx", "head"),
        P("ctx", "head"),
        P("ctx", "head"),
        P("head", "ctx"),
        P("ctx", "head"),
        P("ctx", "head"),
        P("ctx"),
        P(),
        P("ctx", None, None),
        P("ctx", None, "head"),
        P(),
        P(),
        P(),
    )
    out_specs = P("head", "ctx")
    return jax.shard_map(shards, mesh=mesh, in_specs=in_specs, out_specs=out_specs, check_vma=False)
```

time: 131 us -> 123 us (0.939)
  waiting for transfers between devices: 9.52 us -> 5.37 us
  local copies, waits for them, and re-layouts: 6.13 us -> 4.58 us
    all_to_all x1, waiting for transfers between devices: 9.52 us -> 5.37 us  [shards(): blocks = lax.all_to_all(packed, 'ctx', 0, 0, tiled=True)]
    pallas_call x1, Pallas kernels: 5.78 us -> 4.3 us  [shards(): call(attention_kernel, jax.ShapeDtypeStruct((total_rows, query_columns +...]
    pallas_call x3 -> x4, Pallas kernels: 1.98 us -> 3.05 us  [the longest x1 1.59 us: shards(): call(pack_kernel, jax.ShapeDtypeStruct((ctx_count, head_rows + 8, LANES),...]
    unnamed x32 -> x30, local copies, waits for them, and re-layouts: 5.47 us -> 4.58 us
  transfers between devices with their start and end apart: 1 -> 1, of which waited for: 1 -> 1; matrix products, arithmetic and copies ran while one was open for 1% -> 0% of each run, Pallas kernels for 0% -> 0%
where the time goes in v2:
time: 123 us
  blocking collectives  91.3 us (74%)
  starting transfers between devices  11.9 us (10%)
  Pallas kernels  8.98 us (7%)
  waiting for transfers between devices  5.37 us (4%)
  local copies, waits for them, and re-layouts  4.58 us (4%)
    all_to_all x1, blocking collectives, shards(): vectors = lax.all_to_all(vectors, 'ctx', 0, 0, tiled=True)  17.4 us
    all_to_all x1, blocking collectives, shards(): lax.all_to_all(attention, 'ctx', 0, 0, tiled=True)  16.3 us
    all_to_all x1, blocking collectives, shards(): lax.all_to_all(parts.reshape(ctx_count, own_rows, query_columns + LANES),...  16.1 us
    all_to_all x1, blocking collectives, shards(): lax.all_to_all(partial.reshape(ctx_count, own_rows, all_columns), 'ctx',...  15.3 us
    all_to_all x1, blocking collectives, shards(): lax.all_to_all(middles, 'head', 0, 0, tiled=True).reshape(total_rows, LANES)  14 us
    all_to_all x1, blocking collectives, shards(): lax.all_to_all(mixed.reshape(head_count, head_rows, LANES), 'head', 0, 0,...  12.2 us
    all_to_all x1, starting transfers between devices, shards(): blocks = lax.all_to_all(packed, 'ctx', 0, 0, tiled=True)  11.9 us
    all_to_all x1, waiting for transfers between devices, shards(): blocks = lax.all_to_all(packed, 'ctx', 0, 0, tiled=True)  5.37 us
  transfers between devices with their start and end apart: 1, of which 1 were waited for; matrix products, arithmetic and copies ran while one was open for 0% of the time, Pallas kernels for 0%

profile of v2, /device:TPU:1, one launch (start us, length us, event | category | flops | bytes accessed | tf_op | source)
XLA Modules:
  0.0 123.0 jit_solution(10799004972127454143)
XLA Ops:
  0.1 1.6 %pack_tokens.1 = bf16[32,40,128]{2,1,0:T(8,128)(2,1)} custom-call(bf16[256,128]{1,0:T(8,128)(2,1)} %tokens.1, bf16[1,128]{1,0:T(2,128)(2,1)} %bitcast.21), custom_call_target="tpu_custom_call" | custom-call | tf_op jit(solution)/shard_map/pack_tokens/pallas_call | solution.py:402
  1.6 11.9 %all-to-all-start = ((bf16[32,40,128]{2,1,0:T(8,128)(2,1)}), bf16[32,40,128]{2,1,0:T(8,128)(2,1)S(1)}, u32[]{:S(2)}, u32[]{:S(2)}) async-start(bf16[32,40,128]{2,1,0:T(8,128)(2,1)} %pack_tokens.1), calls=%async_computation | async-start | bytes 655360 | tf_op jit(solution)/shard_map/all_to_all | solution.py:414
  13.5 0.0 copy-start.3
  13.5 1.2 copy-done.3
  14.8 0.7 copy-done.10
  15.4 0.7 copy-done.11
  16.1 0.7 copy-done.12
  16.8 0.7 copy-done.13
  17.4 0.7 copy-done.14
  18.1 0.2 early.1
  18.3 5.4 %all-to-all-done.blocks = bf16[32,40,128]{2,1,0:T(8,128)(2,1)S(1)} async-done(((bf16[32,40,128]{2,1,0:T(8,128)(2,1)}), bf16[32,40,128]{2,1,0:T(8,128)(2,1)S(1)}, u32[]{:S(2)}, u32[]{:S(2)}) %all-to-all-start) | async-done | bytes 327712 | tf_op jit(solution)/shard_map/all_to_all | solution.py:414
  23.7 1.1 adapter_middle.1
  24.9 14.0 %all_to_all.35 = f32[8,32,128]{2,1,0:T(8,128)S(1)} all-to-all(f32[8,32,128]{2,1,0:T(8,128)S(1)} %adapter_middle.1), channel_id=1, replica_groups=mesh['ctx'=32,'head'=8] {'head'}, dimensions={0} | all-to-all | bytes 262144 | tf_op jit(solution)/shard_map/all_to_all | solution.py:435
  38.9 1.1 project.1
  40.1 15.3 %all_to_all.36.parts = bf16[32,8,768]{2,1,0:T(8,128)(2,1)S(1)} all-to-all(bf16[32,8,768]{2,1,0:T(8,128)(2,1)S(1)} %bitcast.16), channel_id=1, replica_groups=mesh['ctx'=32,'head'=8] {'ctx'}, dimensions={0} | all-to-all | bytes 786432 | tf_op jit(solution)/shard_map/all_to_all | solution.py:452
  55.3 0.1 sum_projections.1
  55.4 17.4 %all_to_all.37.vectors = bf16[32,8,512]{2,1,0:T(8,128)(2,1)S(1)} all-to-all(bf16[32,8,512]{2,1,0:T(8,128)(2,1)S(1)} %get-tuple-element.15), channel_id=1, replica_groups=mesh['ctx'=32,'head'=8] {'ctx'}, dimensions={0} | all-to-all | bytes 524288 | tf_op jit(solution)/shard_map/all_to_all | solution.py:464
  72.9 4.3 %attention.1 = bf16[256,640]{1,0:T(8,128)(2,1)S(1)} custom-call(s32[8,128]{1,0:T(8,128)S(1)} %get-tuple-element.11.ranges, bf16[32,8,512]{2,1,0:T(8,128)(2,1)S(1)} %all_to_all.37.vectors, f32[8,256]{1,0:T(8,128)S(1)} %get-tuple-element.16.own_pair, bf16[8192,128]{1,0:T(8,128)(2,1)S(1)} %copy-done.1, bf16[8192,128]{1,0:T(8,128)(2,1)S(1)} %copy-done.2), custom_call_target="tpu_custom_call" | custom-call | tf_op jit(solution)/shard_map/attention/pallas_call | solution.py:466
  77.2 16.1 %all_to_all.38.parts = bf16[32,8,640]{2,1,0:T(8,128)(2,1)S(1)} all-to-all(bf16[32,8,640]{2,1,0:T(8,128)(2,1)S(1)} %bitcast.17), channel_id=1, replica_groups=mesh['ctx'=32,'head'=8] {'ctx'}, dimensions={0} | all-to-all | bytes 655360 | tf_op jit(solution)/shard_map/all_to_all | solution.py:480
  93.2 0.5 combine.1
  93.7 16.3 %all_to_all.39 = bf16[32,8,512]{2,1,0:T(8,128)(2,1)S(1)} all-to-all(bf16[32,8,512]{2,1,0:T(8,128)(2,1)S(1)} %combine.1), channel_id=1, replica_groups=mesh['ctx'=32,'head'=8] {'ctx'}, dimensions={0} | all-to-all | bytes 524288 | tf_op jit(solution)/shard_map/all_to_all | solution.py:489
  110.0 0.2 fusion
  110.3 12.2 %all_to_all.40 = f32[8,32,128]{2,1,0:T(8,128)S(1)} all-to-all(f32[8,32,128]{2,1,0:T(8,128)S(1)} %fusion), channel_id=1, replica_groups=mesh['ctx'=32,'head'=8] {'head'}, dimensions={0} | all-to-all | bytes 262144 | tf_op jit(solution)/shard_map/all_to_all | solution.py:491
  122.4 0.6 reduce_sum.9
  (23 shorter events, 0.0 us)
Async XLA Ops:
  0.0 110.0 %copy-start = (bf16[512,128]{1,0:T(8,128)(2,1)S(1)}, bf16[512,128]{1,0:T(8,128)(2,1)}, u32[]{:S(2)}) copy-start(bf16[512,128]{1,0:T(8,128)(2,1)} %param.20) | copy-start | bytes 393220
  0.0 38.9 %copy-start.4 = (bf16[256,128]{1,0:T(8,128)(2,1)S(1)}, bf16[256,128]{1,0:T(8,128)(2,1)}, u32[]{:S(2)}) copy-start(bf16[256,128]{1,0:T(8,128)(2,1)} %tokens.1) | copy-start | bytes 196612
  0.0 38.9 %copy-start.9 = (bf16[128]{0:T(256)(128)(2,1)S(1)}, bf16[128]{0:T(256)(128)(2,1)}, u32[]{:S(2)}) copy-start(bf16[128]{0:T(256)(128)(2,1)} %param.16) | copy-start | bytes 772
  0.0 38.9 %copy-start.6 = (bf16[2,64,512]{2,1,0:T(8,128)(2,1)S(1)}, bf16[2,64,512]{2,1,0:T(8,128)(2,1)}, u32[]{:S(2)}) copy-start(bf16[2,64,512]{2,1,0:T(8,128)(2,1)} %param.26) | copy-start | bytes 393220
  0.0 38.9 %copy-start.8 = (bf16[128,128]{1,0:T(8,128)(2,1)S(1)}, bf16[128,128]{1,0:T(8,128)(2,1)}, u32[]{:S(2)}) copy-start(bf16[128,128]{1,0:T(8,128)(2,1)} %value_matrix.1) | copy-start | bytes 98308
  0.0 38.9 %copy-start.7 = (bf16[128,128]{1,0:T(8,128)(2,1)S(1)}, bf16[128,128]{1,0:T(8,128)(2,1)}, u32[]{:S(2)}) copy-start(bf16[128,128]{1,0:T(8,128)(2,1)} %key_matrix.1) | copy-start | bytes 98308
  0.0 38.9 %copy-start.5 = (bf16[128,512]{1,0:T(8,128)(2,1)S(1)}, bf16[128,512]{1,0:T(8,128)(2,1)}, u32[]{:S(2)}) copy-start(bf16[128,512]{1,0:T(8,128)(2,1)} %query_matrix.1) | copy-start | bytes 393220
  1.6 22.1 %all-to-all-start = ((bf16[32,40,128]{2,1,0:T(8,128)(2,1)}), bf16[32,40,128]{2,1,0:T(8,128)(2,1)S(1)}, u32[]{:S(2)}, u32[]{:S(2)}) async-start(bf16[32,40,128]{2,1,0:T(8,128)(2,1)} %pack_tokens.1), calls=%async_computation | async-start | bytes 655360 | tf_op jit(solution)/shard_map/all_to_all | solution.py:414
  13.5 1.2 copy-start.3
  14.8 0.7 copy-start.10
  15.4 0.7 copy-start.11
  16.1 0.7 copy-start.12
  16.8 0.7 copy-start.13
  17.4 0.7 copy-start.14
  23.7 49.1 %copy-start.1 = (bf16[8192,128]{1,0:T(8,128)(2,1)S(1)}, bf16[8192,128]{1,0:T(8,128)(2,1)}, u32[]{:S(2)}) copy-start(bf16[8192,128]{1,0:T(8,128)(2,1)} %keys.1) | copy-start | bytes 6291460
  23.7 49.1 %copy-start.2 = (bf16[8192,128]{1,0:T(8,128)(2,1)S(1)}, bf16[8192,128]{1,0:T(8,128)(2,1)}, u32[]{:S(2)}) copy-start(bf16[8192,128]{1,0:T(8,128)(2,1)} %values.1) | copy-start | bytes 6291460

commit v3 on v2

--- a/solution.py
+++ b/solution.py
@@ -52,7 +52,7 @@
     return lax.dot_general(a, b, (((1,), (1,)), ((), ())), preferred_element_type=F32)
 
 
-def call(body, out_shape, in_specs, scratch=(), limit=16, flops=0, name=None):
+def call(body, out_shape, in_specs, scratch=(), limit=16, name=None):
     many = isinstance(out_shape, (tuple, list))
     return pl.pallas_call(
         body,
@@ -65,84 +65,93 @@
     )
 
 
-SLOT_ROW, WANTED_ROW = 0, 1
-
-
-def home_of(numbers, wanted_index):
-    return numbers[SLOT_ROW, numbers[WANTED_ROW, wanted_index]]
-
-
-def pack_kernel(tokens_hbm, gain_hbm, out, tokens, gain, arrived):
+PLACE_ROW, STRETCH_ROW, CACHE_ROW, SLOT_ROW, WANTED_ROW = 0, 2, 4, 5, 6
+
+
+def pack_kernel(
+    tokens_hbm,
+    gain_hbm,
+    place_hbm,
+    stretch_hbm,
+    cache_hbm,
+    slot_hbm,
+    wanted_hbm,
+    out,
+    table,
+    tokens,
+    gain,
+    place,
+    stretch,
+    cache,
+    slot,
+    wanted,
+    arrived,
+):
     rows = tokens.shape[0]
     first = pl.multiple_of(lax.axis_index("head") * rows, rows)
+    pairs = (
+        (tokens_hbm.at[pl.ds(first, rows), :], tokens),
+        (gain_hbm, gain),
+        (place_hbm, place),
+        (stretch_hbm, stretch),
+        (cache_hbm, cache),
+        (slot_hbm, slot),
+        (wanted_hbm, wanted),
+    )
     copies = [
-        pltpu.make_async_copy(tokens_hbm.at[pl.ds(first, rows), :], tokens, arrived.at[0]),
-        pltpu.make_async_copy(gain_hbm, gain, arrived.at[1]),
+        pltpu.make_async_copy(source, target, arrived.at[index])
+        for index, (source, target) in enumerate(pairs)
     ]
     for copy in copies:
         copy.start()
-    for copy in copies:
+    for copy in copies[:2]:
         copy.wait()
     gain_rows = jnp.broadcast_to(gain[...].astype(F32), (8, LANES))
     block = jnp.concatenate([tokens[...].astype(F32), gain_rows], axis=0).astype(BF16)
     for target in range(out.shape[0]):
         out[target] = block
-
-
-def early_kernel(
-    place,
-    stretch,
-    cache,
-    slot,
-    wanted,
-    down_hbm,
-    numbers,
-    ranges,
-    places,
-    down,
-    arrived,
-):
+    for copy in copies[2:]:
+        copy.wait()
+    table[...] = jnp.zeros(table.shape, jnp.int32)
+    table[PLACE_ROW : PLACE_ROW + 2, :] = place[...]
+    table[STRETCH_ROW : STRETCH_ROW + 2, :] = stretch[...]
+    for row, part in ((CACHE_ROW, cache), (SLOT_ROW, slot), (WANTED_ROW, wanted)):
+        table[row : row + 1, : part.shape[1]] = part[...]
+
+
+def early_kernel(numbers, table, down_hbm, ranges, uses_first, uses_second, down, arrived):
     copy = pltpu.make_async_copy(down_hbm, down, arrived)
     copy.start()
-    numbers[...] = jnp.zeros(numbers.shape, jnp.int32)
-    for row, part in ((SLOT_ROW, slot), (WANTED_ROW, wanted)):
-        numbers[row : row + 1, : part.shape[1]] = part[...]
-    parts = place.shape[0]
+    parts = uses_first.shape[0] // LANES
+    first_home = lax.axis_index("ctx") * 2
     for part in range(parts):
-        places[part * LANES : (part + 1) * LANES, :] = column_of(place[part : part + 1, :])
+        place = column_of(table[PLACE_ROW + part : PLACE_ROW + part + 1, :])
+        rows = slice(part * LANES, (part + 1) * LANES)
+        for stored, target in enumerate((uses_first, uses_second)):
+            used = jnp.zeros(place.shape, F32)
+            for wanted_index in range(NEED):
+                match = numbers[SLOT_ROW, numbers[WANTED_ROW, wanted_index]] == first_home + stored
+                used = jnp.where((place == float(wanted_index)) & match, 1.0, used)
+            target[rows, :] = used
 
     def wide(row):
-        return jnp.broadcast_to(row.astype(F32), (LANES, LANES))
-
-    cache_row = jnp.concatenate(
-        [cache[...], jnp.zeros((1, LANES - cache.shape[1]), jnp.int32)], axis=1
-    )
-    uppers = [cache_row] + [stretch[part : part + 1, :] for part in range(parts)]
-    counts = [jnp.zeros((1, LANES), F32) for _ in range(1 + len(uppers))]
+        return jnp.broadcast_to(table[row : row + 1, :].astype(F32), (LANES, LANES))
+
+    counts = [jnp.zeros((1, LANES), F32) for _ in range(2 + parts)]
     for part in range(parts):
-        column = column_of(stretch[part : part + 1, :])
-        below = jnp.where(column < wide(cache_row), 1.0, 0.0)
+        row = STRETCH_ROW + part
+        column = column_of(table[row : row + 1, :])
+        below = jnp.where(column < wide(CACHE_ROW), 1.0, 0.0)
         counts[0] = counts[0] + jnp.sum(below, axis=0, keepdims=True)
-        for index, row in enumerate(uppers):
-            below = jnp.where(column <= wide(row), 1.0, 0.0)
+        for index, upper in enumerate([CACHE_ROW] + [STRETCH_ROW + k for k in range(parts)]):
+            below = jnp.where(column <= wide(upper), 1.0, 0.0)
             counts[1 + index] = counts[1 + index] + jnp.sum(below, axis=0, keepdims=True)
     counts.append(jnp.zeros((8 - len(counts), LANES), F32))
     ranges[...] = jnp.concatenate(counts, axis=0).astype(jnp.int32)
     copy.wait()
 
 
-def adapter_choice(numbers, place, first_home):
-    use_first = jnp.zeros(place.shape, jnp.bool_)
-    use_second = jnp.zeros(place.shape, jnp.bool_)
-    for wanted_index in range(NEED):
-        home = home_of(numbers, wanted_index)
-        here = place == float(wanted_index)
-        use_first = use_first | (here & (home == first_home))
-        use_second = use_second | (here & (home == first_home + 1))
-    return use_first, use_second
-
-
-def middle_kernel(numbers, places, blocks, down, out, flat):
+def middle_kernel(uses_first, uses_second, blocks, down, out, flat):
     rows = flat.shape[0]
     squares = jnp.zeros((rows, LANES), F32)
     for source in range(blocks.shape[0]):
@@ -155,32 +164,38 @@
     inverse = lax.rsqrt(mean + EPSILON)
     middle = contract_last(flat[...], down[...]) * inverse
     first = pl.multiple_of(lax.axis_index("head") * rows, rows)
-    use_first, use_second = adapter_choice(
-        numbers, places[pl.ds(first, rows), :], lax.axis_index("ctx") * 2
-    )
-    picked = jnp.where(
-        use_first, middle, jnp.where(use_second, pltpu.roll(middle, RANK, 1), 0.0)
-    )
-    picked = picked.astype(BF16).astype(F32)
-    packed = jnp.where(
-        lane_iota((rows, LANES)) < RANK, picked, jnp.broadcast_to(inverse, (rows, LANES))
-    )
+    picked = middle * uses_first[pl.ds(first, rows), :]
+    picked = picked + pltpu.roll(middle, RANK, 1) * uses_second[pl.ds(first, rows), :]
+    lanes = lane_iota((rows, LANES))
+    high, mid, low = thirds(jnp.broadcast_to(inverse, (rows, LANES)))
+    tail = jnp.where(
+        lanes == RANK, high, jnp.where(lanes == RANK + 1, mid, jnp.where(lanes == RANK + 2, low, 0.0))
+    )
+    packed = jnp.where(lanes < RANK, picked, tail).astype(BF16)
     for target in range(out.shape[0]):
         out[target] = packed
 
 
 def project_kernel(
-    numbers, places, tokens, gain, middles, query_matrix, key_matrix, value_matrix, up, out
+    uses_first,
+    uses_second,
+    tokens,
+    gain,
+    middles,
+    query_matrix,
+    key_matrix,
+    value_matrix,
+    up,
+    out,
 ):
     scaled = (tokens[...].astype(F32) * gain[...].astype(F32)).astype(BF16)
-    packed = middles[...]
+    packed = middles[...].astype(F32)
     lanes = lane_iota(packed.shape)
-    inverse = packed[:, RANK : RANK + 1]
-    use_first, use_second = adapter_choice(numbers, places[...], lax.axis_index("ctx") * 2)
+    inverse = jnp.sum(
+        jnp.where((lanes >= RANK) & (lanes < RANK + 3), packed, 0.0), axis=1, keepdims=True
+    )
     spread = jnp.where(
-        lanes < RANK,
-        jnp.where(use_first, packed, 0.0),
-        jnp.where(use_second, pltpu.roll(packed, RANK, 1), 0.0),
+        lanes < RANK, packed * uses_first[...], pltpu.roll(packed, RANK, 1) * uses_second[...]
     ).astype(BF16)
     columns = up.shape[1]
     change = jnp.dot(spread, up[...], preferred_element_type=F32)
@@ -272,7 +287,7 @@
     own_scores = jnp.where(allowed, own_scores * SCORE_SCALE, LOWEST)
     raise_peaks(own_start, own_scores)
 
-    unroll = 32
+    unroll = 64
 
     def score_step(step, carry):
         found = []
@@ -281,8 +296,7 @@
             start, begin, end = window_of(block)
             key_block = keys[pl.ds(pl.multiple_of(block * SPAN, SPAN), SPAN), :]
             result = contract_last(load(queries, start).astype(BF16), key_block)
-            position = window_row + start
-            allowed = (position >= begin) & (position < end)
+            allowed = (window_row >= begin - start) & (window_row < end - start)
             result = jnp.where(allowed, result * SCORE_SCALE, LOWEST)
             scores[block] = result
             found.append((start, result))
@@ -399,48 +413,57 @@
     slot = adapter_store_slot.reshape(1, adapter_store_slot.shape[0])
     wanted = adapter_wanted_list.reshape(1, NEED)
     gain = input_norm_gain.reshape(1, LANES)
-    packed = call(
+    packed, table = call(
         pack_kernel,
-        jax.ShapeDtypeStruct((ctx_count, head_rows + 8, LANES), BF16),
-        [HBM, HBM],
+        (
+            jax.ShapeDtypeStruct((ctx_count, head_rows + 8, LANES), BF16),
+            jax.ShapeDtypeStruct((8, LANES), jnp.int32),
+        ),
+        [HBM] * 7,
         [
             pltpu.VMEM((head_rows, LANES), BF16),
             pltpu.VMEM((1, LANES), BF16),
-            pltpu.SemaphoreType.DMA((2,)),
+            pltpu.VMEM(place.shape, jnp.int32),
+            pltpu.VMEM(stretch.shape, jnp.int32),
+            pltpu.VMEM(cache.shape, jnp.int32),
+            pltpu.VMEM(slot.shape, jnp.int32),
+            pltpu.VMEM(wanted.shape, jnp.int32),
+            pltpu.SemaphoreType.DMA((7,)),
         ],
         limit=60,
         name="pack_tokens",
-    )(tokens, gain)
+    )(tokens, gain, place, stretch, cache, slot, wanted)
     blocks = lax.all_to_all(packed, "ctx", 0, 0, tiled=True)
     all_columns = query_columns + 2 * HEAD_WIDTH
-    numbers, ranges, places, down = call(
+    mask = jax.ShapeDtypeStruct((total_rows, LANES), F32)
+    ranges, uses_first, uses_second, down = call(
         early_kernel,
         (
             jax.ShapeDtypeStruct((8, LANES), jnp.int32),
-            jax.ShapeDtypeStruct((8, LANES), jnp.int32),
-            jax.ShapeDtypeStruct((total_rows, LANES), F32),
+            mask,
+            mask,
             jax.ShapeDtypeStruct(down.shape, BF16),
         ),
-        [VMEM] * 5 + [HBM],
+        [SMEM, VMEM, HBM],
         [pltpu.SemaphoreType.DMA],
         name="early",
-    )(place, stretch, cache, slot, wanted, down)
+    )(table, table, down)
     middles = call(
         middle_kernel,
-        jax.ShapeDtypeStruct((head_count, head_rows, LANES), F32),
-        [SMEM] + [VMEM] * 3,
+        jax.ShapeDtypeStruct((head_count, head_rows, LANES), BF16),
+        [VMEM] * 4,
         [pltpu.VMEM((head_rows, MODEL_WIDTH), BF16)],
         name="adapter_middle",
-    )(numbers, places, blocks, down)
+    )(uses_first, uses_second, blocks, down)
     middles = lax.all_to_all(middles, "head", 0, 0, tiled=True).reshape(total_rows, LANES)
     partial = call(
         project_kernel,
         jax.ShapeDtypeStruct((total_rows, all_columns), BF16),
-        [SMEM] + [VMEM] * 8,
+        [VMEM] * 9,
         name="project",
     )(
-        numbers,
-        places,
+        uses_first,
+        uses_second,
         tokens,
         gain,
         middles,
@@ -488,8 +511,9 @@
     )(parts)
     attention = lax.all_to_all(attention, "ctx", 0, 0, tiled=True).reshape(total_rows, query_columns)
     mixed = jnp.dot(attention, output_matrix, preferred_element_type=F32)
-    mixed = lax.all_to_all(mixed.reshape(head_count, head_rows, LANES), "head", 0, 0, tiled=True)
-    return jnp.sum(mixed, axis=0).astype(BF16)
+    mixed = mixed.astype(BF16).reshape(head_count, head_rows, LANES)
+    mixed = lax.all_to_all(mixed, "head", 0, 0, tiled=True)
+    return jnp.sum(mixed.astype(F32), axis=0).astype(BF16)
 
 
 def solution(mesh):

time: 123 us -> 120 us (0.976)
  local copies, waits for them, and re-layouts: 4.58 us -> 1.94 us
  waiting for transfers between devices: 5.37 us -> 7.36 us
  blocking collectives: 91.3 us -> 89.6 us
    unnamed x30 -> x22, local copies, waits for them, and re-layouts: 4.58 us -> 1.94 us
    all_to_all x1, waiting for transfers between devices: 5.37 us -> 7.36 us  [shards(): blocks = lax.all_to_all(packed, 'ctx', 0, 0, tiled=True)]
  transfers between devices with their start and end apart: 1 -> 1, of which waited for: 1 -> 1; matrix products, arithmetic and copies ran while one was open for 0% -> 0% of each run, Pallas kernels for 0% -> 1%
where the time goes in v3:
time: 120 us
  blocking collectives  89.6 us (75%)
  starting transfers between devices  11.9 us (10%)
  Pallas kernels  7.79 us (6%)
  waiting for transfers between devices  7.36 us (6%)
  local copies, waits for them, and re-layouts  1.94 us (2%)
    all_to_all x1, blocking collectives, shards(): vectors = lax.all_to_all(vectors, 'ctx', 0, 0, tiled=True)  17.3 us
    all_to_all x1, blocking collectives, shards(): lax.all_to_all(parts.reshape(ctx_count, own_rows, query_columns + LANES),...  16 us
    all_to_all x1, blocking collectives, shards(): lax.all_to_all(attention, 'ctx', 0, 0, tiled=True)  15.7 us
    all_to_all x1, blocking collectives, shards(): lax.all_to_all(partial.reshape(ctx_count, own_rows, all_columns), 'ctx',...  15.5 us
    all_to_all x1, blocking collectives, shards(): lax.all_to_all(middles, 'head', 0, 0, tiled=True).reshape(total_rows, LANES)  13.6 us
    all_to_all x1, starting transfers between devices, shards(): blocks = lax.all_to_all(packed, 'ctx', 0, 0, tiled=True)  11.9 us
    all_to_all x1, blocking collectives, shards(): mixed = lax.all_to_all(mixed, 'head', 0, 0, tiled=True)  11.5 us
    all_to_all x1, waiting for transfers between devices, shards(): blocks = lax.all_to_all(packed, 'ctx', 0, 0, tiled=True)  7.36 us
  transfers between devices with their start and end apart: 1, of which 1 were waited for; matrix products, arithmetic and copies ran while one was open for 0% of the time, Pallas kernels for 1%

profile of v3, /device:TPU:1, one launch (start us, length us, event | category | flops | bytes accessed | tf_op | source)
XLA Modules:
  0.0 119.6 jit_solution(1567115869598143799)
XLA Ops:
  0.1 1.6 %pack_tokens.1 = (bf16[32,40,128]{2,1,0:T(8,128)(2,1)}, s32[8,128]{1,0:T(8,128)}) custom-call(bf16[256,128]{1,0:T(8,128)(2,1)} %tokens.1, bf16[1,128]{1,0:T(2,128)(2,1)} %bitcast.21, s32[2,128]{1,0:T(2,128)} %bitcast.24, s32[2,128]{1,0:T(2,128)} %bitcast.25, s32[1,64]{1,0:T(1,128)} %bitcast.26, s32[1,64]{1,0:T(1,128)} %bitcast.27, s32[1,4]{1,0:T(1,128)} %bitcast.28), custom_call_target="tpu_custom_call" | custom-call | tf_op jit(solution)/shard_map/pack_tokens/pallas_call | solution.py:416
  1.7 11.9 %all-to-all-start = ((bf16[32,40,128]{2,1,0:T(8,128)(2,1)}), bf16[32,40,128]{2,1,0:T(8,128)(2,1)S(1)}, u32[]{:S(2)}, u32[]{:S(2)}) async-start(bf16[32,40,128]{2,1,0:T(8,128)(2,1)} %get-tuple-element.17), calls=%async_computation | async-start | bytes 655360 | tf_op jit(solution)/shard_map/all_to_all | solution.py:436
  13.6 0.0 copy-start.3
  13.6 1.2 %copy-done.3 = bf16[2,64,4096]{2,1,0:T(8,128)(2,1)S(1)} copy-done((bf16[2,64,4096]{2,1,0:T(8,128)(2,1)S(1)}, bf16[2,64,4096]{2,1,0:T(8,128)(2,1)}, u32[]{:S(2)}) %copy-start.3) | copy-done | bytes 1048600
  14.8 0.7 copy-done.9
  15.5 0.9 early.1
  16.4 7.4 %all-to-all-done.blocks = bf16[32,40,128]{2,1,0:T(8,128)(2,1)S(1)} async-done(((bf16[32,40,128]{2,1,0:T(8,128)(2,1)}), bf16[32,40,128]{2,1,0:T(8,128)(2,1)S(1)}, u32[]{:S(2)}, u32[]{:S(2)}) %all-to-all-start) | async-done | bytes 327712 | tf_op jit(solution)/shard_map/all_to_all | solution.py:436
  23.8 0.5 adapter_middle.1
  24.3 13.6 %all_to_all.35 = bf16[8,32,128]{2,1,0:T(8,128)(2,1)S(1)} all-to-all(bf16[8,32,128]{2,1,0:T(8,128)(2,1)S(1)} %adapter_middle.1), channel_id=1, replica_groups=mesh['ctx'=32,'head'=8] {'head'}, dimensions={0} | all-to-all | bytes 131072 | tf_op jit(solution)/shard_map/all_to_all | solution.py:458
  37.9 0.0 copy-done.8
  37.9 0.0 copy-done.7
  37.9 0.0 copy-done.5
  37.9 0.4 project.1
  38.3 15.5 %all_to_all.36.parts = bf16[32,8,768]{2,1,0:T(8,128)(2,1)S(1)} all-to-all(bf16[32,8,768]{2,1,0:T(8,128)(2,1)S(1)} %bitcast.16), channel_id=1, replica_groups=mesh['ctx'=32,'head'=8] {'ctx'}, dimensions={0} | all-to-all | bytes 786432 | tf_op jit(solution)/shard_map/all_to_all | solution.py:475
  53.8 0.1 sum_projections.1
  53.9 17.3 %all_to_all.37.vectors = bf16[32,8,512]{2,1,0:T(8,128)(2,1)S(1)} all-to-all(bf16[32,8,512]{2,1,0:T(8,128)(2,1)S(1)} %get-tuple-element.19), channel_id=1, replica_groups=mesh['ctx'=32,'head'=8] {'ctx'}, dimensions={0} | all-to-all | bytes 524288 | tf_op jit(solution)/shard_map/all_to_all | solution.py:487
  71.2 0.0 copy-done.2
  71.2 3.8 %attention.1 = bf16[256,640]{1,0:T(8,128)(2,1)S(1)} custom-call(s32[8,128]{1,0:T(8,128)S(1)} %get-tuple-element.14.ranges, bf16[32,8,512]{2,1,0:T(8,128)(2,1)S(1)} %all_to_all.37.vectors, f32[8,256]{1,0:T(8,128)S(1)} %get-tuple-element.20.own_pair, bf16[8192,128]{1,0:T(8,128)(2,1)S(1)} %copy-done.1, bf16[8192,128]{1,0:T(8,128)(2,1)S(1)} %copy-done.2), custom_call_target="tpu_custom_call" | custom-call | tf_op jit(solution)/shard_map/attention/pallas_call | solution.py:489
  74.9 16.0 %all_to_all.38.parts = bf16[32,8,640]{2,1,0:T(8,128)(2,1)S(1)} all-to-all(bf16[32,8,640]{2,1,0:T(8,128)(2,1)S(1)} %bitcast.17), channel_id=1, replica_groups=mesh['ctx'=32,'head'=8] {'ctx'}, dimensions={0} | all-to-all | bytes 655360 | tf_op jit(solution)/shard_map/all_to_all | solution.py:503
  90.9 0.5 combine.1
  91.5 15.7 %all_to_all.39 = bf16[32,8,512]{2,1,0:T(8,128)(2,1)S(1)} all-to-all(bf16[32,8,512]{2,1,0:T(8,128)(2,1)S(1)} %combine.1), channel_id=1, replica_groups=mesh['ctx'=32,'head'=8] {'ctx'}, dimensions={0} | all-to-all | bytes 524288 | tf_op jit(solution)/shard_map/all_to_all | solution.py:512
  107.2 0.2 convolution_convert_fusion
  107.4 11.5 %all_to_all.40 = bf16[8,32,128]{2,1,0:T(8,128)(2,1)S(1)} all-to-all(bf16[8,32,128]{2,1,0:T(8,128)(2,1)S(1)} %bitcast.23), channel_id=1, replica_groups=mesh['ctx'=32,'head'=8] {'head'}, dimensions={0} | all-to-all | bytes 131072 | tf_op jit(solution)/shard_map/all_to_all | solution.py:515
  118.9 0.6 reduce_sum.12
  (15 shorter events, 0.0 us)
Async XLA Ops:
  0.0 107.2 %copy-start = (bf16[512,128]{1,0:T(8,128)(2,1)S(1)}, bf16[512,128]{1,0:T(8,128)(2,1)}, u32[]{:S(2)}) copy-start(bf16[512,128]{1,0:T(8,128)(2,1)} %param.20) | copy-start | bytes 393220
  0.0 37.9 %copy-start.4 = (bf16[256,128]{1,0:T(8,128)(2,1)S(1)}, bf16[256,128]{1,0:T(8,128)(2,1)}, u32[]{:S(2)}) copy-start(bf16[256,128]{1,0:T(8,128)(2,1)} %tokens.1) | copy-start | bytes 196612
  0.0 37.9 %copy-start.10 = (bf16[128]{0:T(256)(128)(2,1)S(1)}, bf16[128]{0:T(256)(128)(2,1)}, u32[]{:S(2)}) copy-start(bf16[128]{0:T(256)(128)(2,1)} %param.16) | copy-start | bytes 772
  0.0 37.9 %copy-start.6 = (bf16[2,64,512]{2,1,0:T(8,128)(2,1)S(1)}, bf16[2,64,512]{2,1,0:T(8,128)(2,1)}, u32[]{:S(2)}) copy-start(bf16[2,64,512]{2,1,0:T(8,128)(2,1)} %param.26) | copy-start | bytes 393220
  0.0 37.9 %copy-start.8 = (bf16[128,128]{1,0:T(8,128)(2,1)S(1)}, bf16[128,128]{1,0:T(8,128)(2,1)}, u32[]{:S(2)}) copy-start(bf16[128,128]{1,0:T(8,128)(2,1)} %value_matrix.1) | copy-start | bytes 98308
  0.0 37.9 %copy-start.7 = (bf16[128,128]{1,0:T(8,128)(2,1)S(1)}, bf16[128,128]{1,0:T(8,128)(2,1)}, u32[]{:S(2)}) copy-start(bf16[128,128]{1,0:T(8,128)(2,1)} %key_matrix.1) | copy-start | bytes 98308
  0.0 37.9 %copy-start.5 = (bf16[128,512]{1,0:T(8,128)(2,1)S(1)}, bf16[128,512]{1,0:T(8,128)(2,1)}, u32[]{:S(2)}) copy-start(bf16[128,512]{1,0:T(8,128)(2,1)} %query_matrix.1) | copy-start | bytes 393220
  1.7 22.1 %all-to-all-start = ((bf16[32,40,128]{2,1,0:T(8,128)(2,1)}), bf16[32,40,128]{2,1,0:T(8,128)(2,1)S(1)}, u32[]{:S(2)}, u32[]{:S(2)}) async-start(bf16[32,40,128]{2,1,0:T(8,128)(2,1)} %get-tuple-element.17), calls=%async_computation | async-start | bytes 655360 | tf_op jit(solution)/shard_map/all_to_all | solution.py:436
  13.6 1.2 %copy-start.3 = (bf16[2,64,4096]{2,1,0:T(8,128)(2,1)S(1)}, bf16[2,64,4096]{2,1,0:T(8,128)(2,1)}, u32[]{:S(2)}) copy-start(bf16[2,64,4096]{2,1,0:T(8,128)(2,1)} %param.25) | copy-start | bytes 3145732
  14.8 0.7 copy-start.9
  23.8 47.4 %copy-start.1 = (bf16[8192,128]{1,0:T(8,128)(2,1)S(1)}, bf16[8192,128]{1,0:T(8,128)(2,1)}, u32[]{:S(2)}) copy-start(bf16[8192,128]{1,0:T(8,128)(2,1)} %keys.1) | copy-start | bytes 6291460
  23.8 47.4 %copy-start.2 = (bf16[8192,128]{1,0:T(8,128)(2,1)S(1)}, bf16[8192,128]{1,0:T(8,128)(2,1)}, u32[]{:S(2)}) copy-start(bf16[8192,128]{1,0:T(8,128)(2,1)} %values.1) | copy-start | bytes 6291460

commit v4 on v3

--- a/solution.py
+++ b/solution.py
@@ -15,6 +15,7 @@
 GROUP = 4
 RANK = 64
 WINDOW = 24
+BATCH = 16
 
 LOWEST = -1e30
 FLOOR = -1e29
@@ -52,13 +53,13 @@
     return lax.dot_general(a, b, (((1,), (1,)), ((), ())), preferred_element_type=F32)
 
 
-def call(body, out_shape, in_specs, scratch=(), limit=16, name=None):
+def call(body, out_shape, in_specs, scratch=(), limit=16, name=None, out_specs=None):
     many = isinstance(out_shape, (tuple, list))
     return pl.pallas_call(
         body,
         out_shape=out_shape,
         in_specs=in_specs,
-        out_specs=[VMEM] * len(out_shape) if many else VMEM,
+        out_specs=out_specs or ([VMEM] * len(out_shape) if many else VMEM),
         scratch_shapes=list(scratch),
         compiler_params=pltpu.CompilerParams(vmem_limit_bytes=limit * 1024 * 1024),
         name=name,
@@ -76,7 +77,7 @@
     cache_hbm,
     slot_hbm,
     wanted_hbm,
-    out,
+    out_hbm,
     table,
     tokens,
     gain,
@@ -85,7 +86,9 @@
     cache,
     slot,
     wanted,
+    blocks,
     arrived,
+    sent,
 ):
     rows = tokens.shape[0]
     first = pl.multiple_of(lax.axis_index("head") * rows, rows)
@@ -108,8 +111,15 @@
         copy.wait()
     gain_rows = jnp.broadcast_to(gain[...].astype(F32), (8, LANES))
     block = jnp.concatenate([tokens[...].astype(F32), gain_rows], axis=0).astype(BF16)
-    for target in range(out.shape[0]):
-        out[target] = block
+    batch = blocks.shape[0]
+    for target in range(batch):
+        blocks[target] = block
+    sends = [
+        pltpu.make_async_copy(blocks, out_hbm.at[pl.ds(index * batch, batch)], sent.at[index])
+        for index in range(out_hbm.shape[0] // batch)
+    ]
+    for copy in sends:
+        copy.start()
     for copy in copies[2:]:
         copy.wait()
     table[...] = jnp.zeros(table.shape, jnp.int32)
@@ -117,6 +127,8 @@
     table[STRETCH_ROW : STRETCH_ROW + 2, :] = stretch[...]
     for row, part in ((CACHE_ROW, cache), (SLOT_ROW, slot), (WANTED_ROW, wanted)):
         table[row : row + 1, : part.shape[1]] = part[...]
+    for copy in sends:
+        copy.wait()
 
 
 def early_kernel(numbers, table, down_hbm, ranges, uses_first, uses_second, down, arrived):
@@ -287,14 +299,11 @@
     own_scores = jnp.where(allowed, own_scores * SCORE_SCALE, LOWEST)
     raise_peaks(own_start, own_scores)
 
-    unroll = 64
-
-    def score_step(step, carry):
+    def score_blocks(first):
         found = []
-        for k in range(unroll):
-            block = step * unroll + k
+        for block in range(first, first + BATCH):
             start, begin, end = window_of(block)
-            key_block = keys[pl.ds(pl.multiple_of(block * SPAN, SPAN), SPAN), :]
+            key_block = keys[block * SPAN : (block + 1) * SPAN, :]
             result = contract_last(load(queries, start).astype(BF16), key_block)
             allowed = (window_row >= begin - start) & (window_row < end - start)
             result = jnp.where(allowed, result * SCORE_SCALE, LOWEST)
@@ -302,9 +311,9 @@
             found.append((start, result))
         for start, result in found:
             raise_peaks(start, result)
-        return carry
-
-    lax.fori_loop(0, block_count // unroll, score_step, 0)
+
+    for first in range(0, block_count, BATCH):
+        score_blocks(first)
     for g in range(GROUP):
         highest = jnp.max(peaks[g], axis=1, keepdims=True)
         peaks[g] = jnp.broadcast_to(jnp.maximum(highest, FLOOR), (total_rows, LANES))
@@ -316,20 +325,19 @@
         jnp.dot(own_weights.astype(BF16), new_values, preferred_element_type=F32),
     )
 
-    def value_step(step, carry):
+    def value_blocks(first):
         found = []
-        for k in range(unroll):
-            block = step * unroll + k
+        for block in range(first, first + BATCH):
             start, begin, end = window_of(block)
             weights = jnp.exp2(scores[block] - load(peaks, start))
-            value_block = values[pl.ds(pl.multiple_of(block * SPAN, SPAN), SPAN), :]
+            value_block = values[block * SPAN : (block + 1) * SPAN, :]
             product = jnp.dot(weights.astype(BF16), value_block, preferred_element_type=F32)
             found.append((start, weights, product))
         for start, weights, product in found:
             add_up(start, weights, product)
-        return carry
-
-    lax.fori_loop(0, block_count // unroll, value_step, 0)
+
+    for first in range(0, block_count, BATCH):
+        value_blocks(first)
 
     quarter = lanes % GROUP
     peak_all = jnp.zeros((total_rows, LANES), F32)
@@ -428,10 +436,13 @@
             pltpu.VMEM(cache.shape, jnp.int32),
             pltpu.VMEM(slot.shape, jnp.int32),
             pltpu.VMEM(wanted.shape, jnp.int32),
+            pltpu.VMEM((8, head_rows + 8, LANES), BF16),
             pltpu.SemaphoreType.DMA((7,)),
+            pltpu.SemaphoreType.DMA((ctx_count // 8,)),
         ],
         limit=60,
         name="pack_tokens",
+        out_specs=[HBM, VMEM],
     )(tokens, gain, place, stretch, cache, slot, wanted)
     blocks = lax.all_to_all(packed, "ctx", 0, 0, tiled=True)
     all_columns = query_columns + 2 * HEAD_WIDTH

time: 120 us -> 121 us (level)
  no operation moved by 1% of the time
where the time goes in v4:
time: 121 us; the launch traced here: 120 us
  blocking collectives  89.7 us (74%)
  starting transfers between devices  11.9 us (10%)
  Pallas kernels  8.35 us (7%)
  waiting for transfers between devices  7.36 us (6%)
  local copies, waits for them, and re-layouts  1.94 us (2%)
    all_to_all x1, blocking collectives, shards(): vectors = lax.all_to_all(vectors, 'ctx', 0, 0, tiled=True)  17.3 us
    all_to_all x1, blocking collectives, shards(): lax.all_to_all(attention, 'ctx', 0, 0, tiled=True)  16 us
    all_to_all x1, blocking collectives, shards(): lax.all_to_all(parts.reshape(ctx_count, own_rows, query_columns + LANES),...  16 us
    all_to_all x1, blocking collectives, shards(): lax.all_to_all(partial.reshape(ctx_count, own_rows, all_columns), 'ctx',...  15.5 us
    all_to_all x1, blocking collectives, shards(): lax.all_to_all(middles, 'head', 0, 0, tiled=True).reshape(total_rows, LANES)  13.6 us
    all_to_all x1, starting transfers between devices, shards(): blocks = lax.all_to_all(packed, 'ctx', 0, 0, tiled=True)  11.9 us
    all_to_all x1, blocking collectives, shards(): mixed = lax.all_to_all(mixed, 'head', 0, 0, tiled=True)  11.5 us
    all_to_all x1, waiting for transfers between devices, shards(): blocks = lax.all_to_all(packed, 'ctx', 0, 0, tiled=True)  7.36 us
  transfers between devices with their start and end apart: 1, of which 1 were waited for; matrix products, arithmetic and copies ran while one was open for 0% of the time, Pallas kernels for 1%

profile of v4, /device:TPU:1, one launch (start us, length us, event | category | flops | bytes accessed | tf_op | source)
XLA Modules:
  0.0 120.2 jit_solution(660029613534020314)
XLA Ops:
  0.0 0.0 copy-start
  0.0 0.0 copy-start.6
  0.0 0.0 copy-start.8
  0.1 2.2 %pack_tokens.1 = (bf16[32,40,128]{2,1,0:T(8,128)(2,1)}, s32[8,128]{1,0:T(8,128)}) custom-call(bf16[256,128]{1,0:T(8,128)(2,1)} %tokens.1, bf16[1,128]{1,0:T(2,128)(2,1)} %bitcast.21, s32[2,128]{1,0:T(2,128)} %bitcast.24, s32[2,128]{1,0:T(2,128)} %bitcast.25, s32[1,64]{1,0:T(1,128)} %bitcast.26, s32[1,64]{1,0:T(1,128)} %bitcast.27, s32[1,4]{1,0:T(1,128)} %bitcast.28), custom_call_target="tpu_custom_call" | custom-call | tf_op jit(solution)/shard_map/pack_tokens/pallas_call | solution.py:424
  2.3 11.9 %all-to-all-start = ((bf16[32,40,128]{2,1,0:T(8,128)(2,1)}), bf16[32,40,128]{2,1,0:T(8,128)(2,1)S(1)}, u32[]{:S(2)}, u32[]{:S(2)}) async-start(bf16[32,40,128]{2,1,0:T(8,128)(2,1)} %get-tuple-element.17), calls=%async_computation | async-start | bytes 655360 | tf_op jit(solution)/shard_map/all_to_all | solution.py:447
  14.2 0.0 copy-start.3
  14.2 1.2 %copy-done.3 = bf16[2,64,4096]{2,1,0:T(8,128)(2,1)S(1)} copy-done((bf16[2,64,4096]{2,1,0:T(8,128)(2,1)S(1)}, bf16[2,64,4096]{2,1,0:T(8,128)(2,1)}, u32[]{:S(2)}) %copy-start.3) | copy-done | bytes 1048600
  15.4 0.7 copy-done.9
  16.1 0.9 early.1
  17.0 7.4 %all-to-all-done.blocks = bf16[32,40,128]{2,1,0:T(8,128)(2,1)S(1)} async-done(((bf16[32,40,128]{2,1,0:T(8,128)(2,1)}), bf16[32,40,128]{2,1,0:T(8,128)(2,1)S(1)}, u32[]{:S(2)}, u32[]{:S(2)}) %all-to-all-start) | async-done | bytes 327712 | tf_op jit(solution)/shard_map/all_to_all | solution.py:447
  24.3 0.5 adapter_middle.1
  24.9 13.6 %all_to_all.35 = bf16[8,32,128]{2,1,0:T(8,128)(2,1)S(1)} all-to-all(bf16[8,32,128]{2,1,0:T(8,128)(2,1)S(1)} %adapter_middle.1), channel_id=1, replica_groups=mesh['ctx'=32,'head'=8] {'head'}, dimensions={0} | all-to-all | bytes 131072 | tf_op jit(solution)/shard_map/all_to_all | solution.py:469
  38.5 0.4 project.1
  38.9 15.5 %all_to_all.36.parts = bf16[32,8,768]{2,1,0:T(8,128)(2,1)S(1)} all-to-all(bf16[32,8,768]{2,1,0:T(8,128)(2,1)S(1)} %bitcast.16), channel_id=1, replica_groups=mesh['ctx'=32,'head'=8] {'ctx'}, dimensions={0} | all-to-all | bytes 786432 | tf_op jit(solution)/shard_map/all_to_all | solution.py:486
  54.4 0.1 sum_projections.1
  54.5 17.3 %all_to_all.37.vectors = bf16[32,8,512]{2,1,0:T(8,128)(2,1)S(1)} all-to-all(bf16[32,8,512]{2,1,0:T(8,128)(2,1)S(1)} %get-tuple-element.19), channel_id=1, replica_groups=mesh['ctx'=32,'head'=8] {'ctx'}, dimensions={0} | all-to-all | bytes 524288 | tf_op jit(solution)/shard_map/all_to_all | solution.py:498
  71.7 0.0 copy-done.2
  71.8 3.7 %attention.1 = bf16[256,640]{1,0:T(8,128)(2,1)S(1)} custom-call(s32[8,128]{1,0:T(8,128)S(1)} %get-tuple-element.14.ranges, bf16[32,8,512]{2,1,0:T(8,128)(2,1)S(1)} %all_to_all.37.vectors, f32[8,256]{1,0:T(8,128)S(1)} %get-tuple-element.20.own_pair, bf16[8192,128]{1,0:T(8,128)(2,1)S(1)} %copy-done.1, bf16[8192,128]{1,0:T(8,128)(2,1)S(1)} %copy-done.2), custom_call_target="tpu_custom_call" | custom-call | tf_op jit(solution)/shard_map/attention/pallas_call | solution.py:500
  75.5 16.0 %all_to_all.38.parts = bf16[32,8,640]{2,1,0:T(8,128)(2,1)S(1)} all-to-all(bf16[32,8,640]{2,1,0:T(8,128)(2,1)S(1)} %bitcast.17), channel_id=1, replica_groups=mesh['ctx'=32,'head'=8] {'ctx'}, dimensions={0} | all-to-all | bytes 655360 | tf_op jit(solution)/shard_map/all_to_all | solution.py:514
  91.5 0.5 combine.1
  92.0 16.0 %all_to_all.39 = bf16[32,8,512]{2,1,0:T(8,128)(2,1)S(1)} all-to-all(bf16[32,8,512]{2,1,0:T(8,128)(2,1)S(1)} %combine.1), channel_id=1, replica_groups=mesh['ctx'=32,'head'=8] {'ctx'}, dimensions={0} | all-to-all | bytes 524288 | tf_op jit(solution)/shard_map/all_to_all | solution.py:523
  107.9 0.2 convolution_convert_fusion
  108.2 11.5 %all_to_all.40 = bf16[8,32,128]{2,1,0:T(8,128)(2,1)S(1)} all-to-all(bf16[8,32,128]{2,1,0:T(8,128)(2,1)S(1)} %bitcast.23), channel_id=1, replica_groups=mesh['ctx'=32,'head'=8] {'head'}, dimensions={0} | all-to-all | bytes 131072 | tf_op jit(solution)/shard_map/all_to_all | solution.py:526
  119.6 0.6 reduce_sum.12
  (15 shorter events, 0.0 us)
Async XLA Ops:
  0.0 107.9 %copy-start = (bf16[512,128]{1,0:T(8,128)(2,1)S(1)}, bf16[512,128]{1,0:T(8,128)(2,1)}, u32[]{:S(2)}) copy-start(bf16[512,128]{1,0:T(8,128)(2,1)} %param.20) | copy-start | bytes 393220
  0.0 38.5 %copy-start.4 = (bf16[256,128]{1,0:T(8,128)(2,1)S(1)}, bf16[256,128]{1,0:T(8,128)(2,1)}, u32[]{:S(2)}) copy-start(bf16[256,128]{1,0:T(8,128)(2,1)} %tokens.1) | copy-start | bytes 196612
  0.0 38.5 %copy-start.10 = (bf16[128]{0:T(256)(128)(2,1)S(1)}, bf16[128]{0:T(256)(128)(2,1)}, u32[]{:S(2)}) copy-start(bf16[128]{0:T(256)(128)(2,1)} %param.16) | copy-start | bytes 772
  0.0 38.5 %copy-start.6 = (bf16[2,64,512]{2,1,0:T(8,128)(2,1)S(1)}, bf16[2,64,512]{2,1,0:T(8,128)(2,1)}, u32[]{:S(2)}) copy-start(bf16[2,64,512]{2,1,0:T(8,128)(2,1)} %param.26) | copy-start | bytes 393220
  0.0 38.5 %copy-start.8 = (bf16[128,128]{1,0:T(8,128)(2,1)S(1)}, bf16[128,128]{1,0:T(8,128)(2,1)}, u32[]{:S(2)}) copy-start(bf16[128,128]{1,0:T(8,128)(2,1)} %value_matrix.1) | copy-start | bytes 98308
  0.0 38.5 %copy-start.7 = (bf16[128,128]{1,0:T(8,128)(2,1)S(1)}, bf16[128,128]{1,0:T(8,128)(2,1)}, u32[]{:S(2)}) copy-start(bf16[128,128]{1,0:T(8,128)(2,1)} %key_matrix.1) | copy-start | bytes 98308
  0.0 38.5 %copy-start.5 = (bf16[128,512]{1,0:T(8,128)(2,1)S(1)}, bf16[128,512]{1,0:T(8,128)(2,1)}, u32[]{:S(2)}) copy-start(bf16[128,512]{1,0:T(8,128)(2,1)} %query_matrix.1) | copy-start | bytes 393220
  2.3 22.1 %all-to-all-start = ((bf16[32,40,128]{2,1,0:T(8,128)(2,1)}), bf16[32,40,128]{2,1,0:T(8,128)(2,1)S(1)}, u32[]{:S(2)}, u32[]{:S(2)}) async-start(bf16[32,40,128]{2,1,0:T(8,128)(2,1)} %get-tuple-element.17), calls=%async_computation | async-start | bytes 655360 | tf_op jit(solution)/shard_map/all_to_all | solution.py:447
  14.2 1.2 %copy-start.3 = (bf16[2,64,4096]{2,1,0:T(8,128)(2,1)S(1)}, bf16[2,64,4096]{2,1,0:T(8,128)(2,1)}, u32[]{:S(2)}) copy-start(bf16[2,64,4096]{2,1,0:T(8,128)(2,1)} %param.25) | copy-start | bytes 3145732
  15.4 0.7 copy-start.9
  24.3 47.4 %copy-start.1 = (bf16[8192,128]{1,0:T(8,128)(2,1)S(1)}, bf16[8192,128]{1,0:T(8,128)(2,1)}, u32[]{:S(2)}) copy-start(bf16[8192,128]{1,0:T(8,128)(2,1)} %keys.1) | copy-start | bytes 6291460
  24.3 47.4 %copy-start.2 = (bf16[8192,128]{1,0:T(8,128)(2,1)S(1)}, bf16[8192,128]{1,0:T(8,128)(2,1)}, u32[]{:S(2)}) copy-start(bf16[8192,128]{1,0:T(8,128)(2,1)} %values.1) | copy-start | bytes 6291460
